TPU v7x, 128 devices: a whole 4x4x4 slice. The times are simulated.
128 devices in a mesh: wide: 32 (over x, z_hi, y), narrow: 4 (over z_lo, core).
Axes of the slice: x: 4, y: 4, z: 4 (z_hi: 2, z_lo: 2; z = z_hi * 2 + z_lo), core: 2. Of those that a mesh axis runs over, the one named last changes fastest.
Arguments:
- ratio_field: float32 [1024, 1024, 128], P('narrow', 'wide'), may hold values from 0.3 to 3
- estimate: float32 [1024, 1024, 128], P('narrow', 'wide'), may hold values from 0.1 to 10
- psf_spectrum: float32 [1024, 1024, 128], P(None, ('wide', 'narrow')), may hold values from 0.05 to 1
Outputs:
- new_estimate: float32 [1024, 1024, 128], P('narrow', 'wide')
All inputs are finite; a program needn't handle non-finite values.
Results may differ from a plain program's by a relative error of at most 0.00013.
Values sent between devices are 32-bit elements; how exact they have to be, the bound alone decides.
No kernel may reach another device: no remote copies, remote signals or barrier semaphores. Data moves between devices by JAX's collectives and lax.ppermute only.
A program may use at most 128 MiB of HBM per device.

v0:
```python
import jax
import jax.numpy as jnp
from jax import lax
from jax.sharding import PartitionSpec as P


def cosine_table(length):
    freq = lax.iota(jnp.float32, length)[:, None]
    cells = lax.iota(jnp.float32, length)[None, :]
    scale = jnp.where(freq == 0, jnp.sqrt(1.0 / length), jnp.sqrt(2.0 / length)).astype(jnp.float32)
    return scale * jnp.cos(jnp.pi * (cells + 0.5) * freq / length)


def local(ratio_field, estimate, psf_spectrum):
    highest = lax.Precision.HIGHEST
    wide_count = lax.axis_size("wide")
    narrow_count = lax.axis_size("narrow")
    z_length = ratio_field.shape[2]
    table_z = cosine_table(z_length)
    volume = jnp.einsum("xyz,cz->xyc", ratio_field, table_z, precision=highest)
    volume = lax.all_to_all(volume, "wide", split_axis=0, concat_axis=1, tiled=True)
    x_slab = volume.shape[0]
    y_span = volume.shape[1]
    y_part = y_span // (wide_count * narrow_count)
    table_y = cosine_table(y_span)
    volume = jnp.einsum("xyz,by->xbz", volume, table_y, precision=highest)
    volume = volume.reshape(1, 1, x_slab, wide_count, narrow_count, y_part, z_length)
    volume = lax.all_to_all(
        lax.all_to_all(volume, "wide", split_axis=3, concat_axis=1, tiled=True),
        "narrow",
        split_axis=4,
        concat_axis=0,
        tiled=True,
    )
    x_span = narrow_count * wide_count * x_slab
    volume = volume.reshape(x_span, y_part, z_length)
    table_x = cosine_table(x_span)
    volume = jnp.einsum("xyz,ax->ayz", volume, table_x, precision=highest)
    volume = volume * psf_spectrum
    volume = jnp.einsum("ayz,ax->xyz", volume, table_x, precision=highest)
    volume = volume.reshape(narrow_count, wide_count, x_slab, 1, 1, y_part, z_length)
    volume = lax.all_to_all(
        lax.all_to_all(volume, "wide", split_axis=1, concat_axis=3, tiled=True),
        "narrow",
        split_axis=0,
        concat_axis=4,
        tiled=True,
    )
    volume = volume.reshape(x_slab, y_span, z_length)
    volume = jnp.einsum("xbz,by->xyz", volume, table_y, precision=highest)
    volume = lax.all_to_all(volume, "wide", split_axis=1, concat_axis=0, tiled=True)
    volume = jnp.einsum("xyc,cz->xyz", volume, table_z, precision=highest)
    return estimate * volume


def solution(mesh):
    placed = (
        P("narrow", "wide", None),
        P("narrow", "wide", None),
        P(None, ("wide", "narrow"), None),
    )
    return jax.shard_map(
        local, mesh=mesh, in_specs=placed, out_specs=P("narrow", "wide", None), check_vma=False
    )
```

profile of v0, /device:TPU:0, one launch (start us, length us, event | category | flops | bytes accessed | tf_op | source)
XLA Modules:
  0.0 503.4 jit_solution(7247284828388034964)
XLA Ops:
  0.0 10.1 %fusion.14 = f32[256,32,128]{0,2,1:T(8,128)} fusion(f32[256,32,128]{2,1,0:T(8,128)} %param.3, f32[128]{0:T(128)S(1)} %get-tuple-element.6, f32[128]{0:T(128)S(1)} %get-tuple-element.5), kind=kOutput, calls=%fused_computation.17 | convolution fusion | flops 1610661888 | bytes 8389632 | tf_op jit(solution)/shard_map/xyz,cz->xyc/dot_general | solution.py:20
  10.1 5.5 %copy.23 = f32[256,32,128]{2,1,0:T(8,128)} copy(f32[256,32,128]{0,2,1:T(8,128)} %fusion.14) | data formatting | bytes 8388608 | tf_op jit(solution)/shard_map/xyz,cz->xyc/dot_general | solution.py:20
  15.6 10.8 %all-to-all-start = ((f32[256,32,128]{2,1,0:T(8,128)}), f32[256,32,128]{2,1,0:T(8,128)}, u32[]{:S(2)}, u32[]{:S(2)}) async-start(f32[256,32,128]{2,1,0:T(8,128)} %copy.23), calls=%async_computation | async-start | bytes 8388608 | tf_op jit(solution)/shard_map/all_to_all | solution.py:21
  26.5 60.8 %all-to-all-done = f32[256,32,128]{2,1,0:T(8,128)} async-done(((f32[256,32,128]{2,1,0:T(8,128)}), f32[256,32,128]{2,1,0:T(8,128)}, u32[]{:S(2)}, u32[]{:S(2)}) %all-to-all-start) | async-done | bytes 4194336 | tf_op jit(solution)/shard_map/all_to_all | solution.py:21
  87.3 2.8 copy.24
  90.1 27.5 %fusion.2 = f32[1024,8,128]{2,0,1:T(8,128)S(1)} fusion(f32[8,1024,128]{2,1,0:T(8,128)S(1)} %bitcast.64, f32[1024]{0:T(1024)S(1)} %get-tuple-element.7, f32[1024]{0:T(1024)S(1)} %get-tuple-element.8), kind=kOutput, calls=%fused_computation.2 | convolution fusion | flops 12888047616 | bytes 8396800 | tf_op jit(solution)/shard_map/xyz,by->xbz/dot_general | solution.py:26
  117.6 0.6 copy.26
  118.2 58.7 %all_to_all.102 = f32[1,1,8,32,4,8,128]{6,5,2,4,1,0,3:T(8,128)S(1)} all-to-all(f32[1,1,8,32,4,8,128]{6,5,2,4,1,0,3:T(8,128)S(1)} %copy.26), channel_id=1, replica_groups=mesh['wide'=32,'narrow'=4] {'wide'}, dimensions={3} | all-to-all | bytes 8388608 | tf_op jit(solution)/shard_map/all_to_all | solution.py:29
  176.9 0.6 copy.27
  177.4 50.7 %all_to_all.103 = f32[1,32,8,1,4,8,128]{6,5,2,1,3,0,4:T(8,128)S(1)} all-to-all(f32[1,32,8,1,4,8,128]{6,5,2,1,3,0,4:T(8,128)S(1)} %copy.27), channel_id=1, replica_groups=mesh['wide'=32,'narrow'=4] {'narrow'}, dimensions={4} | all-to-all | bytes 8388608 | tf_op jit(solution)/shard_map/all_to_all | solution.py:28
  228.2 0.0 copy-start.1
  228.2 38.0 %fusion.4 = f32[1024,8,128]{2,0,1:T(8,128)S(1)} fusion(f32[1024,8,128]{2,1,0:T(8,128)S(1)} %bitcast.66, f32[1024]{0:T(1024)S(1)} %get-tuple-element.7, f32[1024]{0:T(1024)S(1)} %get-tuple-element.8), kind=kOutput, calls=%fused_computation.4 | convolution fusion | flops 12888047616 | bytes 8396800 | tf_op jit(solution)/shard_map/xyz,ax->ayz/dot_general | solution.py:38
  266.1 0.0 copy-done.1
  266.2 28.6 %fusion.8 = f32[1024,8,128]{2,0,1:T(8,128)S(1)} fusion(f32[1024,8,128]{2,0,1:T(8,128)S(1)} %fusion.4, f32[1024,8,128]{2,1,0:T(8,128)S(1)} %copy-done.1, f32[1024]{0:T(1024)S(1)} %get-tuple-element.7, f32[1024]{0:T(1024)S(1)} %get-tuple-element.8), kind=kOutput, calls=%fused_computation.8 | convolution fusion | flops 12889096192 | bytes 12591104 | tf_op jit(solution)/shard_map/ayz,ax->xyz/dot_general | solution.py:40
  294.8 0.6 copy.31
  295.4 55.9 %all_to_all.104 = f32[4,32,8,1,1,8,128]{6,2,0,5,4,3,1:T(8,128)S(1)} all-to-all(f32[4,32,8,1,1,8,128]{6,2,0,5,4,3,1:T(8,128)S(1)} %copy.31), channel_id=1, replica_groups=mesh['wide'=32,'narrow'=4] {'wide'}, dimensions={1} | all-to-all | bytes 8388608 | tf_op jit(solution)/shard_map/all_to_all | solution.py:43
  351.2 0.5 copy.32
  351.7 50.7 %all_to_all.105 = f32[4,1,8,32,1,8,128]{6,2,3,5,4,1,0:T(8,128)S(1)} all-to-all(f32[4,1,8,32,1,8,128]{6,2,3,5,4,1,0:T(8,128)S(1)} %copy.32), channel_id=1, replica_groups=mesh['wide'=32,'narrow'=4] {'narrow'}, dimensions={0} | all-to-all | bytes 8388608 | tf_op jit(solution)/shard_map/all_to_all | solution.py:42
  402.5 2.4 copy.33
  404.9 27.9 %fusion.17 = f32[8,1024,128]{2,1,0:T(8,128)S(1)} fusion(f32[8,1024,128]{2,1,0:T(8,128)S(1)} %bitcast.63, f32[1024]{0:T(1024)S(1)} %get-tuple-element.7, f32[1024]{0:T(1024)S(1)} %get-tuple-element.8), kind=kOutput, calls=%fused_computation.18 | convolution fusion | flops 12888047616 | bytes 8396800 | tf_op jit(solution)/shard_map/xbz,by->xyz/dot_general | solution.py:50
  432.8 2.4 copy.34
  435.2 0.0 copy-start
  435.3 56.0 %all_to_all.106 = f32[8,1024,128]{2,0,1:T(8,128)S(1)} all-to-all(f32[8,1024,128]{2,0,1:T(8,128)S(1)} %copy.34), channel_id=1, replica_groups=mesh['wide'=32,'narrow'=4] {'wide'}, dimensions={1} | all-to-all | bytes 8388608 | tf_op jit(solution)/shard_map/all_to_all | solution.py:51
  491.2 0.0 copy-done
  491.2 7.4 %copy_multiply_fusion = f32[256,32,128]{2,0,1:T(8,128)S(1)} fusion(f32[256,32,128]{2,1,0:T(8,128)S(1)} %copy-done, f32[8,32,32,128]{3,0,2,1:T(8,128)S(1)} %bitcast.59, f32[128]{0:T(128)S(1)} %get-tuple-element.6, f32[128]{0:T(128)S(1)} %get-tuple-element.5), kind=kOutput, calls=%fused_computation.10 | convolution fusion | flops 1611710464 | bytes 12583936 | tf_op jit(solution)/shard_map/xyc,cz->xyz/dot_general | solution.py:52
  498.6 4.4 copy.37
  (2 shorter events, 0.0 us)
Async XLA Ops:
  15.6 71.6 %all-to-all-start = ((f32[256,32,128]{2,1,0:T(8,128)}), f32[256,32,128]{2,1,0:T(8,128)}, u32[]{:S(2)}, u32[]{:S(2)}) async-start(f32[256,32,128]{2,1,0:T(8,128)} %copy.23), calls=%async_computation | async-start | bytes 8388608 | tf_op jit(solution)/shard_map/all_to_all | solution.py:21
  228.2 38.0 %copy-start.1 = (f32[1024,8,128]{2,1,0:T(8,128)S(1)}, f32[1024,8,128]{2,1,0:T(8,128)}, u32[]{:S(2)}) copy-start(f32[1024,8,128]{2,1,0:T(8,128)} %param.5) | copy-start | bytes 12582916
  435.2 56.0 %copy-start = (f32[256,32,128]{2,1,0:T(8,128)S(1)}, f32[256,32,128]{2,1,0:T(8,128)}, u32[]{:S(2)}) copy-start(f32[256,32,128]{2,1,0:T(8,128)} %param.4) | copy-start | bytes 12582916
where the time goes:
time: 509 us; the launch traced here: 503 us
  blocking collectives  272 us (53%)
  matrix products  140 us (28%)
  waiting for transfers between devices  60.8 us (12%)
  local copies, waits for them, and re-layouts  19.8 us (4%)
  starting transfers between devices  10.8 us (2%)
    all_to_all x1, waiting for transfers between devices, local(): lax.all_to_all(volume, 'wide', split_axis=0, concat_axis=1, tiled=True)  60.8 us
    all_to_all x1, blocking collectives, local(): lax.all_to_all(volume, 'wide', split_axis=3, concat_axis=1, tiled=True)  58.7 us
    all_to_all x1, blocking collectives, local(): lax.all_to_all(volume, 'wide', split_axis=1, concat_axis=0, tiled=True)  56 us
    all_to_all x1, blocking collectives, local(): lax.all_to_all(volume, 'wide', split_axis=1, concat_axis=3, tiled=True)  55.9 us
    all_to_all x1, blocking collectives, local(): lax.all_to_all(lax.all_to_all(volume, 'wide', split_axis=3, concat_axis=1...  50.7 us
    all_to_all x1, blocking collectives, local(): lax.all_to_all(lax.all_to_all(volume, 'wide', split_axis=1, concat_axis=3...  50.7 us
    dot_general x1, matrix products, local(): volume = jnp.einsum('xyz,ax->ayz', volume, table_x, precision=highest)  38 us
    dot_general x1, matrix products, local(): volume = jnp.einsum('ayz,ax->xyz', volume, table_x, precision=highest)  28.6 us
  transfers between devices with their start and end apart: 1, of which 1 were waited for; matrix products, arithmetic and copies ran while one was open for 0% of the time, Pallas kernels for 0%

commit v1 on v0

v1 whole, which is shorter than its diff:
```python
import functools

import jax
import jax.numpy as jnp
import ml_dtypes
import numpy as np
from jax import lax
from jax.experimental import pallas as pl
from jax.experimental.pallas import tpu as pltpu
from jax.sharding import PartitionSpec as P

F32 = jnp.float32
BF16 = jnp.bfloat16
ALL = ("x", "zh", "y", "zl", "core")
LIMIT = 40 * 1024 * 1024


def cosine_table(length):
    freq = np.arange(length, dtype=np.float32)[:, None]
    cells = np.arange(length, dtype=np.float32)[None, :]
    angle = np.float32(np.pi) * (cells + np.float32(0.5)) * freq / np.float32(length)
    scale = np.where(freq == 0, np.sqrt(np.float32(1.0 / length)), np.sqrt(np.float32(2.0 / length)))
    return scale.astype(np.float32) * np.cos(angle.astype(np.float64)).astype(np.float32)


def halves(table):
    high = table.astype(ml_dtypes.bfloat16)
    low = (table - high.astype(np.float32)).astype(ml_dtypes.bfloat16)
    return high, low


def split(value):
    high = value.astype(BF16)
    return high, (value - high.astype(F32)).astype(BF16)


def dot3(a_high, a_low, b_high, b_low):
    dot = functools.partial(jnp.dot, preferred_element_type=F32)
    return dot(a_high, b_high) + dot(a_high, b_low) + dot(a_low, b_high)


def device_id(px, zr, py, core):
    zr = zr % 4
    return (((px * 2 + zr // 2) * 4 + py) * 2 + zr % 2) * 2 + core


def moves(step, flip):
    return [
        (device_id(px, zr, py, core), device_id(px, zr + step, py, core ^ flip))
        for px in range(4)
        for py in range(4)
        for zr in range(4)
        for core in range(2)
    ]


def y_forward_kernel(order, volume, high, low, *rest):
    outs, rows = rest[:4], rest[4]
    v_high, v_low = split(volume[...].reshape(1024, 256))
    rows[...] = dot3(high[...], low[...], v_high, v_low)
    for dest in range(4):
        for q in range(2):
            begin = pl.multiple_of(order[dest * 2 + q] * 128, 128)
            outs[dest][q, 0] = rows[pl.ds(begin, 128), :]


def y_forward(order, volume, high, low, slot):
    part = jax.ShapeDtypeStruct((2, 2, 128, 256), F32)
    whole = pl.BlockSpec((1024, 1024), lambda c: (0, 0))
    return pl.pallas_call(
        y_forward_kernel,
        grid=(2,),
        in_specs=[
            pl.BlockSpec(memory_space=pltpu.SMEM),
            pl.BlockSpec((32, 1, 32, 256), lambda c: (0, 2 * slot + c, 0, 0)),
            whole,
            whole,
        ],
        out_specs=[pl.BlockSpec((2, 1, 128, 256), lambda c: (0, c, 0, 0))] * 4,
        out_shape=[part] * 4,
        scratch_shapes=[pltpu.VMEM((1024, 256), F32)],
        compiler_params=pltpu.CompilerParams(vmem_limit_bytes=LIMIT),
        cost_estimate=pl.CostEstimate(flops=3 * 2**30, bytes_accessed=8 * 2**20, transcendentals=0),
        name="y_forward",
    )(order, volume, high, low)


def x_forward_kernel(order, *refs):
    parts, (high, low, out, v_high, v_low) = refs[:4], refs[4:]

    @pl.when(pl.program_id(0) == 0)
    def _():
        for k in range(4):
            v_high[k], v_low[k] = split(parts[k][...].reshape(512, 256))

    total = None
    for k in range(4):
        block = order[k]
        term = dot3(v_high[k], v_low[k], high[block], low[block])
        total = term if total is None else total + term
    out[...] = total.reshape(2, 2, 128, 256)


def x_forward(order, parts, high, low):
    table = pl.BlockSpec((4, 256, 256), lambda a: (0, 0, a))
    return pl.pallas_call(
        x_forward_kernel,
        grid=(4,),
        in_specs=[pl.BlockSpec(memory_space=pltpu.SMEM)]
        + [pl.BlockSpec((2, 2, 128, 256), lambda a: (0, 0, 0, 0))] * 4
        + [table, table],
        out_specs=pl.BlockSpec((2, 2, 128, 256), lambda a: (0, 0, 0, a)),
        out_shape=jax.ShapeDtypeStruct((2, 2, 128, 1024), F32),
        scratch_shapes=[pltpu.VMEM((4, 512, 256), BF16)] * 2,
        compiler_params=pltpu.CompilerParams(vmem_limit_bytes=LIMIT),
        cost_estimate=pl.CostEstimate(flops=3 * 2**30, bytes_accessed=8 * 2**20, transcendentals=0),
        name="x_forward",
    )(order, *parts, high, low)


def x_inverse_kernel(order, spectrum, psf, high, low, *rest):
    outs, (v_high, v_low) = rest[:4], rest[4:]
    step = pl.program_id(0)

    @pl.when(step == 0)
    def _():
        for q in range(2):
            for c in range(2):
                value = spectrum[q, c] * psf[:, 0, q, c].reshape(128, 1024)
                rows = pl.ds((q * 2 + c) * 128, 128)
                v_high[rows, :], v_low[rows, :] = split(value)

    result = dot3(v_high[...], v_low[...], high[0], low[0]).reshape(2, 2, 128, 256)
    for dest in range(4):

        @pl.when(step == dest)
        def _():
            outs[dest][...] = result


def x_inverse(order, spectrum, psf, high, low, slot):
    part = jax.ShapeDtypeStruct((2, 2, 128, 256), F32)
    table = pl.BlockSpec((1, 1024, 256), lambda d, order: (order[d], 0, 0))
    return pl.pallas_call(
        x_inverse_kernel,
        grid_spec=pltpu.PrefetchScalarGridSpec(
            num_scalar_prefetch=1,
            grid=(4,),
            in_specs=[
                pl.BlockSpec((2, 2, 128, 1024), lambda d, order: (0, 0, 0, 0)),
                pl.BlockSpec((16, 1, 2, 2, 8, 1024), lambda d, order: (0, slot, 0, 0, 0, 0)),
                table,
                table,
            ],
            out_specs=[pl.BlockSpec((2, 2, 128, 256), lambda d, order: (0, 0, 0, 0))] * 4,
            scratch_shapes=[pltpu.VMEM((512, 1024), BF16)] * 2,
        ),
        out_shape=[part] * 4,
        compiler_params=pltpu.CompilerParams(vmem_limit_bytes=LIMIT),
        cost_estimate=pl.CostEstimate(flops=3 * 2**30, bytes_accessed=10 * 2**20, transcendentals=0),
        name="x_inverse",
    )(order, spectrum, psf, high, low)


def y_inverse_kernel(order, *refs):
    parts, (high, low), (out, v_high, v_low) = refs[:4], refs[4:6], refs[-3:]
    for dest in range(4):
        for q in range(2):
            rows = pl.ds(pl.multiple_of(order[dest * 2 + q] * 128, 128), 128)
            v_high[rows, :], v_low[rows, :] = split(parts[dest][q, 0])
    result = dot3(high[...], low[...], v_high[...], v_low[...])
    out[...] = result.reshape(32, 1, 32, 256)


def y_inverse(order, parts, high, low, slot, into):
    whole = pl.BlockSpec((1024, 1024), lambda c: (0, 0))
    in_specs = [pl.BlockSpec(memory_space=pltpu.SMEM)]
    in_specs += [pl.BlockSpec((2, 1, 128, 256), lambda c: (0, c, 0, 0))] * 4
    in_specs += [whole, whole]
    args = [order, *parts, high, low]
    aliases = {}
    if into is not None:
        in_specs.append(pl.BlockSpec(memory_space=pl.ANY))
        args.append(into)
        aliases = {7: 0}
    return pl.pallas_call(
        y_inverse_kernel,
        grid=(2,),
        in_specs=in_specs,
        out_specs=pl.BlockSpec((32, 1, 32, 256), lambda c: (0, 2 * slot + c, 0, 0)),
        out_shape=jax.ShapeDtypeStruct((32, 4, 32, 256), F32),
        scratch_shapes=[pltpu.VMEM((1024, 256), BF16)] * 2,
        input_output_aliases=aliases,
        compiler_params=pltpu.CompilerParams(vmem_limit_bytes=LIMIT),
        cost_estimate=pl.CostEstimate(flops=3 * 2**30, bytes_accessed=8 * 2**20, transcendentals=0),
        name="y_inverse",
    )(*args)


def local(ratio_field, estimate, psf_spectrum):
    px, zh, py, zl, core = (lax.axis_index(name) for name in ALL)
    ring = 2 * zh + zl
    narrow = 2 * zl + core

    cz = cosine_table(128)
    cz_order = np.array(
        [
            [
                (gx * 4 + gy) * 8 + ((2 * h + low - 1 + side) % 4) * 2 + i
                for gx in range(4)
                for h in range(2)
                for gy in range(4)
                for side in range(2)
                for i in range(2)
            ]
            for low in range(2)
        ]
    )
    table_z = jnp.asarray(cz[cz_order])[zl]
    pick_order = np.array(
        [
            [
                g * 8 + ((r + shift) % 4) * 2 + i
                for shift in (-1, 0, -2, 1)
                for g in range(16)
                for i in range(2)
            ]
            for r in range(4)
        ]
    )
    pick = jnp.asarray(np.eye(128, dtype=np.float32)[pick_order])[ring]
    cy = cosine_table(1024)
    b_order = np.array(
        [
            (((gx * 2 + r // 2) * 4 + gy) * 2 + r % 2) * 16 + k * 8 + j
            for r in range(4)
            for k in range(2)
            for gx in range(4)
            for gy in range(4)
            for j in range(8)
        ]
    )
    y_rows = [jnp.asarray(h) for h in halves(cy[b_order])]
    y_columns = [jnp.asarray(h) for h in halves(np.ascontiguousarray(cy[b_order].T))]
    cx = cosine_table(1024)
    x_rows = [jnp.asarray(h) for h in halves(np.ascontiguousarray(cx.T).reshape(4, 256, 1024))]
    x_columns = [
        jnp.asarray(h) for h in halves(np.ascontiguousarray(cx.reshape(1024, 4, 256).transpose(1, 0, 2)))
    ]

    b_sets = []
    for sign in (-1, 1):
        sets = []
        for near, flip in ((0, 0), (0, 1), (1, 0), (1, 1)):
            for q in range(2):
                place = ring + sign * (1 + q) if near else ring - sign * q
                sets.append((place % 4) * 2 + (core ^ flip))
        b_sets.append(jnp.stack(sets).astype(jnp.int32))
    x_blocks = jnp.stack([narrow ^ d for d in range(4)]).astype(jnp.int32)

    def exchange(lower, upper):
        send = functools.partial(lax.ppermute, axis_name=ALL)
        got_lower = [
            lower[0],
            send(lower[1], perm=moves(0, 1)),
            send(upper[2], perm=moves(1, 0)),
            send(upper[3], perm=moves(1, 1)),
        ]
        got_upper = [
            upper[0],
            send(upper[1], perm=moves(0, 1)),
            send(lower[2], perm=moves(-1, 0)),
            send(lower[3], perm=moves(-1, 1)),
        ]
        return got_lower, got_upper

    volume = jnp.einsum("xyz,cz->cyx", ratio_field, table_z, precision=lax.Precision.HIGH)
    volume = lax.all_to_all(volume, ("x", "zh", "y"), split_axis=0, concat_axis=0, tiled=True)
    volume = volume.reshape(32, 4, 32, 256)

    psf = jnp.einsum("abc,dc->dba", psf_spectrum, pick, precision=lax.Precision.HIGH)
    psf = psf.reshape(4, 16, 2, 8, 1024)
    from_above = lax.ppermute(psf[2], ALL, moves(-1, 0))
    from_below = lax.ppermute(psf[3], ALL, moves(1, 0))
    psf = jnp.stack([jnp.stack([psf[0], from_above], 1), jnp.stack([psf[1], from_below], 1)], 1)
    psf = lax.all_to_all(psf, ("x", "y"), split_axis=0, concat_axis=0, tiled=True)

    lower = y_forward(b_sets[0], volume, *y_rows, 0)
    upper = y_forward(b_sets[1], volume, *y_rows, 1)
    lower, upper = exchange(lower, upper)
    lower = x_forward(x_blocks, lower, *x_rows)
    upper = x_forward(x_blocks, upper, *x_rows)
    lower = x_inverse(x_blocks, lower, psf, *x_columns, 0)
    upper = x_inverse(x_blocks, upper, psf, *x_columns, 1)
    lower, upper = exchange(lower, upper)
    volume = y_inverse(b_sets[0], lower, *y_columns, 0, None)
    volume = y_inverse(b_sets[1], upper, *y_columns, 1, volume)

    volume = volume.reshape(128, 32, 256)
    volume = lax.all_to_all(volume, ("x", "zh", "y"), split_axis=0, concat_axis=0, tiled=True)
    volume = jnp.einsum("cyx,cz->xyz", volume, table_z, precision=lax.Precision.HIGH)
    return estimate * volume


def solution(mesh):
    cut = jax.sharding.Mesh(mesh.devices.reshape(4, 2, 4, 2, 2), ALL)
    wide, narrow = ("x", "zh", "y"), ("zl", "core")
    placed = (P(narrow, wide, None), P(narrow, wide, None), P(None, wide + narrow, None))
    return jax.shard_map(
        local, mesh=cut, in_specs=placed, out_specs=P(narrow, wide, None), check_vma=False
    )
```

time: 509 us -> 312 us (0.61)
  blocking collectives: 272 us -> 0 us
  matrix products: 140 us -> 20.7 us
  waiting for transfers between devices: 60.8 us -> 157 us
  Pallas kernels: 0 us -> 47 us
  starting transfers between devices: 10.8 us -> 45.4 us
  local copies, waits for them, and re-layouts: 19.8 us -> 35.2 us
    all_to_all x5 -> x0, blocking collectives: 272 us -> none  [the longest x1 58.7 us: local(): lax.all_to_all(volume, 'wide', split_axis=3, concat_axis=1, tiled=True)]
    dot_general x6 -> x3, matrix products: 140 us -> 20.7 us  [the longest x1 9.6 us: local(): jnp.einsum('cyx,cz->xyz', volume, table_z, precision=lax.Precision.HIGH)]
    ppermute x0 -> x14, waiting for transfers between devices: none -> 91.2 us  [the longest x1 57.6 us: local(): from_above = lax.ppermute(psf[2], ALL, moves(-1, 0))]
    pallas_call x0 -> x8, Pallas kernels: none -> 47 us  [the longest x2 13.9 us: x_inverse(): pl.pallas_call(x_inverse_kernel, grid_spec=pltpu.PrefetchScalarGridSpec(n...]
    unnamed x4 -> x43, local copies, waits for them, and re-layouts: 0.01 us -> 22.2 us
    all_to_all x1 -> x3, starting transfers between devices: 10.8 us -> 30.8 us  [the longest x2 23 us: local(): lax.all_to_all(volume, ('x', 'zh', 'y'), split_axis=0, concat_axis=0, til...]
    ppermute x0 -> x14, starting transfers between devices: none -> 14.6 us  [the longest x2 5.93 us: exchange(): send(upper[2], perm=moves(1, 0))]
    all_to_all x4 -> x0, local copies, waits for them, and re-layouts: 6.31 us -> none  [the longest x1 2.81 us: local(): lax.all_to_all(volume, 'wide', split_axis=0, concat_axis=1, tiled=True)]
  transfers between devices with their start and end apart: 1 -> 17, of which waited for: 1 -> 10; matrix products, arithmetic and copies ran while one was open for 0% -> 5% of each run, Pallas kernels for 0% -> 11%
where the time goes in v1:
time: 312 us; the launch traced here: 309 us
  waiting for transfers between devices  157 us (50%)
  Pallas kernels  47 us (15%)
  starting transfers between devices  45.4 us (15%)
  local copies, waits for them, and re-layouts  35.2 us (11%)
  matrix products  20.7 us (7%)
    ppermute x1, waiting for transfers between devices, local(): from_above = lax.ppermute(psf[2], ALL, moves(-1, 0))  57.6 us
    all_to_all x2, waiting for transfers between devices, local(): lax.all_to_all(volume, ('x', 'zh', 'y'), split_axis=0, concat_axis=0, til...  57.4 us
    all_to_all x2, starting transfers between devices, local(): lax.all_to_all(volume, ('x', 'zh', 'y'), split_axis=0, concat_axis=0, til...  23 us
    unnamed x43, local copies, waits for them, and re-layouts  22.2 us
    ppermute x2, waiting for transfers between devices, exchange(): send(lower[3], perm=moves(-1, 1))  15.3 us
    pallas_call x2, Pallas kernels, x_inverse(): pl.pallas_call(x_inverse_kernel, grid_spec=pltpu.PrefetchScalarGridSpec(n...  13.9 us
    pallas_call x2, Pallas kernels, x_forward(): pl.pallas_call(x_forward_kernel, grid=(4,), in_specs=[pl.BlockSpec(memory...  12.1 us
    pallas_call x2, Pallas kernels, y_forward(): pl.pallas_call(y_forward_kernel, grid=(2,), in_specs=[pl.BlockSpec(memory...  11.7 us
  transfers between devices with their start and end apart: 17, of which 10 were waited for; matrix products, arithmetic and copies ran while one was open for 5% of the time, Pallas kernels for 11%

profile of v1, /device:TPU:0, one launch (start us, length us, event | category | flops | bytes accessed | tf_op | source)
XLA Modules:
  0.0 308.8 jit_solution(14584193953042485140)
XLA Ops:
  0.0 6.3 %fusion.6 = f32[128,32,256]{2,0,1:T(8,128)S(1)} fusion(f32[256,32,128]{2,1,0:T(8,128)} %param.13, f32[2,128,128]{2,1,0:T(8,128)} %constant.93.clone, s32[]{:T(128)S(6)} %select_n.51), kind=kOutput, calls=%fused_computation.8 | convolution fusion | flops 805306368 | bytes 8454148 | tf_op jit(solution)/shard_map/xyz,cz->cyx/dot_general | solution.py:277
  6.3 4.4 %copy.27 = f32[128,32,256]{2,1,0:T(8,128)} copy(f32[128,32,256]{2,0,1:T(8,128)S(1)} %fusion.6) | data formatting | bytes 8388608 | tf_op jit(solution)/shard_map/xyz,cz->cyx/transpose | solution.py:277
  10.8 10.8 %all-to-all-start = ((f32[128,32,256]{2,1,0:T(8,128)}), f32[128,32,256]{2,1,0:T(8,128)}, u32[]{:S(2)}, u32[]{:S(2)}) async-start(f32[128,32,256]{2,1,0:T(8,128)} %copy.27), calls=%async_computation | async-start | bytes 8388608 | tf_op jit(solution)/shard_map/all_to_all | solution.py:278
  21.6 4.8 %fusion.9 = f32[128,8,1024]{2,0,1:T(8,128)S(1)} fusion(f32[1024,8,128]{2,1,0:T(8,128)} %param.15, f32[4,128,128]{2,1,0:T(8,128)} %constant.94.clone, s32[]{:T(128)S(6)} %select_n.57), kind=kOutput, calls=%fused_computation.9 | convolution fusion | flops 805306368 | bytes 8454148 | tf_op jit(solution)/shard_map/abc,dc->dba/dot_general | solution.py:281
  27.7 3.4 %collective-permute-start.3 = (f32[16,2,8,1024]{3,2,1,0:T(8,128)S(1)}, f32[16,2,8,1024]{3,2,1,0:T(8,128)S(1)}, u32[]{:S(2)}, u32[]{:S(2)}) collective-permute-start(f32[16,2,8,1024]{3,2,1,0:T(8,128)S(1)} %bitcast.48), channel_id=1, source_target_pairs={{0,18},{1,19},{2,0},{3,1},{16,2},{17,3},{18,16},{19,17},{4,22},{5,... | collective-permute-start | bytes 3145736 | tf_op jit(solution)/shard_map/ppermute | solution.py:283
  33.2 57.6 %collective-permute-done.3 = f32[16,2,8,1024]{3,2,1,0:T(8,128)S(1)} collective-permute-done((f32[16,2,8,1024]{3,2,1,0:T(8,128)S(1)}, f32[16,2,8,1024]{3,2,1,0:T(8,128)S(1)}, u32[]{:S(2)}, u32[]{:S(2)}) %collective-permute-start.3) | collective-permute-done | bytes 1048608 | tf_op jit(solution)/shard_map/ppermute | solution.py:283
  92.7 2.3 pad_maximum_fusion
  95.0 7.8 %all-to-all-start.1 = ((f32[16,2,2,2,8,1024]{5,4,3,2,1,0:T(8,128)}), f32[16,2,2,2,8,1024]{5,4,3,2,1,0:T(8,128)}, u32[]{:S(2)}, u32[]{:S(2)}) async-start(f32[16,2,2,2,8,1024]{5,4,3,2,1,0:T(8,128)} %pad_maximum_fusion), calls=%async_computation.1 | async-start | bytes 8388608 | tf_op jit(solution)/shard_map/all_to_all | solution.py:286
  103.1 1.6 copy-done.11
  104.7 5.9 %y_forward.3 = (f32[2,2,128,256]{3,2,1,0:T(8,128)S(1)}, f32[2,2,128,256]{3,2,1,0:T(8,128)S(1)}, f32[2,2,128,256]{3,2,1,0:T(8,128)S(1)}, f32[2,2,128,256]{3,2,1,0:T(8,128)}) custom-call(s32[8]{0:T(128)S(1)} %stack.94.order, f32[32,4,32,256]{3,2,1,0:T(8,128)} %bitcast.16.volume, bf16[1024,1024]{1,0:T(8,128)(2,1)S(1)} %copy-done.11, ...), custom_call_target="tpu_custom_call" | custom-call | flops 3221225472 | bytes 8388608 | tf_op jit(solution)/shard_map/y_forward/pallas_call | solution.py:70
  112.1 5.8 %y_forward.2 = (f32[2,2,128,256]{3,2,1,0:T(8,128)S(1)}, f32[2,2,128,256]{3,2,1,0:T(8,128)}, f32[2,2,128,256]{3,2,1,0:T(8,128)S(1)}, f32[2,2,128,256]{3,2,1,0:T(8,128)S(1)}) custom-call(s32[8]{0:T(128)S(1)} %stack.86.order, f32[32,4,32,256]{3,2,1,0:T(8,128)} %bitcast.16.volume, bf16[1024,1024]{1,0:T(8,128)(2,1)S(1)} %copy-done.11, ...), custom_call_target="tpu_custom_call" | custom-call | flops 3221225472 | bytes 8388608 | tf_op jit(solution)/shard_map/y_forward/pallas_call | solution.py:70
  120.6 5.7 %collective-permute-done.1.refs_2_ = f32[2,2,128,256]{3,2,1,0:T(8,128)S(1)} collective-permute-done((f32[2,2,128,256]{3,2,1,0:T(8,128)S(1)}, f32[2,2,128,256]{3,2,1,0:T(8,128)S(1)}, u32[]{:S(2)}, u32[]{:S(2)}) %collective-permute-start.1) | collective-permute-done | bytes 524320 | tf_op jit(solution)/shard_map/ppermute | solution.py:272
  126.4 7.8 %collective-permute-done.2.refs_3_ = f32[2,2,128,256]{3,2,1,0:T(8,128)} collective-permute-done((f32[2,2,128,256]{3,2,1,0:T(8,128)}, f32[2,2,128,256]{3,2,1,0:T(8,128)}, u32[]{:S(2)}, u32[]{:S(2)}) %collective-permute-start.2) | collective-permute-done | bytes 524320 | tf_op jit(solution)/shard_map/ppermute | solution.py:273
  134.1 1.6 copy-done.7
  138.4 6.2 %x_forward.2.spectrum = f32[2,2,128,1024]{3,2,1,0:T(8,128)S(1)} custom-call(s32[4]{0:T(128)S(1)} %pad_add_fusion.order, f32[2,2,128,256]{3,2,1,0:T(8,128)S(1)} %copy-done.19, f32[2,2,128,256]{3,2,1,0:T(8,128)} %collective-permute-done.refs_1_, f32[2,2,128,256]{3,2,1,0:T(8,128)S(1)} %collective-permute-done.1.refs_2_, ...), custom_call_target="tpu_custom_call" | custom-call | flops 3221225472 | bytes 8388608 | tf_op jit(solution)/shard_map/x_forward/pallas_call | solution.py:106
  146.3 6.0 %x_forward.3.spectrum = f32[2,2,128,1024]{3,2,1,0:T(8,128)S(1)} custom-call(s32[4]{0:T(128)S(1)} %pad_add_fusion.order, f32[2,2,128,256]{3,2,1,0:T(8,128)S(1)} %copy-done.17, f32[2,2,128,256]{3,2,1,0:T(8,128)S(1)} %collective-permute-done.6.refs_1_, f32[2,2,128,256]{3,2,1,0:T(8,128)S(1)} %collective-permute-done.7.refs_2_, ...), custom_call_target="tpu_custom_call" | custom-call | flops 3221225472 | bytes 8388608 | tf_op jit(solution)/shard_map/x_forward/pallas_call | solution.py:106
  153.6 8.6 %all-to-all-done.1.psf = f32[16,2,2,2,8,1024]{5,4,3,2,1,0:T(8,128)} async-done(((f32[16,2,2,2,8,1024]{5,4,3,2,1,0:T(8,128)}), f32[16,2,2,2,8,1024]{5,4,3,2,1,0:T(8,128)}, u32[]{:S(2)}, u32[]{:S(2)}) %all-to-all-start.1) | async-done | bytes 4194336 | tf_op jit(solution)/shard_map/all_to_all | solution.py:286
  167.0 7.0 %x_inverse.2 = (f32[2,2,128,256]{3,2,1,0:T(8,128)S(1)}, f32[2,2,128,256]{3,2,1,0:T(8,128)S(1)}, f32[2,2,128,256]{3,2,1,0:T(8,128)S(1)}, f32[2,2,128,256]{3,2,1,0:T(8,128)S(1)}) custom-call(s32[4]{0:T(128)S(1)} %pad_add_fusion.order, f32[2,2,128,1024]{3,2,1,0:T(8,128)S(1)} %copy-done.13, f32[16,2,2,2,8,1024]{5,4,3,2,1,0:T(8,128)} %all-to-all-done.1.psf, ...), custom_call_target="tpu_custom_call" | custom-call | flops 3221225472 | bytes 10485760 | tf_op jit(solution)/shard_map/x_inverse/pallas_call | solution.py:144
  173.9 5.1 %collective-permute-start.12 = (f32[2,2,128,256]{3,2,1,0:T(8,128)S(1)}, f32[2,2,128,256]{3,2,1,0:T(8,128)S(1)}, u32[]{:S(2)}, u32[]{:S(2)}) collective-permute-start(f32[2,2,128,256]{3,2,1,0:T(8,128)S(1)} %get-tuple-element.35), channel_id=1, source_target_pairs={{0,2},{1,3},{2,16},{3,17},{16,18},{17,19},{18,0},{19,1},{4,6},{5,7... | collective-permute-start | bytes 1572872 | tf_op jit(solution)/shard_map/ppermute | solution.py:266
  179.1 7.0 %x_inverse.3 = (f32[2,2,128,256]{3,2,1,0:T(8,128)S(1)}, f32[2,2,128,256]{3,2,1,0:T(8,128)S(1)}, f32[2,2,128,256]{3,2,1,0:T(8,128)S(1)}, f32[2,2,128,256]{3,2,1,0:T(8,128)S(1)}) custom-call(s32[4]{0:T(128)S(1)} %pad_add_fusion.order, f32[2,2,128,1024]{3,2,1,0:T(8,128)S(1)} %copy-done.15, f32[16,2,2,2,8,1024]{5,4,3,2,1,0:T(8,128)} %all-to-all-done.1.psf, ...), custom_call_target="tpu_custom_call" | custom-call | flops 3221225472 | bytes 10485760 | tf_op jit(solution)/shard_map/x_inverse/pallas_call | solution.py:144
  186.7 2.6 collective-permute-start.9
  189.3 2.3 collective-permute-done.12.refs_2_
  191.6 8.5 %collective-permute-done.13.refs_3_ = f32[2,2,128,256]{3,2,1,0:T(8,128)S(1)} collective-permute-done((f32[2,2,128,256]{3,2,1,0:T(8,128)S(1)}, f32[2,2,128,256]{3,2,1,0:T(8,128)S(1)}, u32[]{:S(2)}, u32[]{:S(2)}) %collective-permute-start.13) | collective-permute-done | bytes 524320 | tf_op jit(solution)/shard_map/ppermute | solution.py:267
  200.1 4.6 %y_inverse.2.refs_6_ = f32[32,4,32,256]{3,2,1,0:T(8,128)S(1)} custom-call(s32[8]{0:T(128)S(1)} %stack.94.order, f32[2,2,128,256]{3,2,1,0:T(8,128)S(1)} %get-tuple-element.33.refs_0_, f32[2,2,128,256]{3,2,1,0:T(8,128)S(1)} %collective-permute-done.11.refs_1_, f32[2,2,128,256]{3,2,1,0:T(8,128)S(1)} %collective-permute-done.12.refs_2_, ...), custom_call_target="tpu_custom_call" | custom-call | flops 3221225472 | bytes 8388608 | tf_op jit(solution)/shard_map/y_inverse/pallas_call | solution.py:186
  204.7 7.6 %collective-permute-done.10.refs_3_ = f32[2,2,128,256]{3,2,1,0:T(8,128)S(1)} collective-permute-done((f32[2,2,128,256]{3,2,1,0:T(8,128)S(1)}, f32[2,2,128,256]{3,2,1,0:T(8,128)S(1)}, u32[]{:S(2)}, u32[]{:S(2)}) %collective-permute-start.10) | collective-permute-done | bytes 524320 | tf_op jit(solution)/shard_map/ppermute | solution.py:273
  212.3 4.6 %y_inverse.3 = f32[32,4,32,256]{3,2,1,0:T(8,128)S(1)} custom-call(s32[8]{0:T(128)S(1)} %stack.86.order, f32[2,2,128,256]{3,2,1,0:T(8,128)S(1)} %get-tuple-element.25.refs_0_, f32[2,2,128,256]{3,2,1,0:T(8,128)S(1)} %collective-permute-done.5.refs_1_, f32[2,2,128,256]{3,2,1,0:T(8,128)S(1)} %collective-permute-done.9.refs_2_, ...), custom_call_target="tpu_custom_call", output_to_operand_aliasing={{}: (7, {})} | custom-call | flops 3221225472 | bytes 8388608 | tf_op jit(solution)/shard_map/y_inverse/pallas_call | solution.py:186
  216.9 2.0 copy-done
  219.0 12.2 %all-to-all-start.2 = ((f32[128,32,256]{2,1,0:T(8,128)}), f32[128,32,256]{2,1,0:T(8,128)}, u32[]{:S(2)}, u32[]{:S(2)}) async-start(f32[128,32,256]{2,1,0:T(8,128)} %bitcast.44), calls=%async_computation.2 | async-start | bytes 8388608 | tf_op jit(solution)/shard_map/all_to_all | solution.py:300
  231.1 5.3 %copy.35 = f32[256,32,128]{0,2,1:T(8,128)} copy(f32[256,32,128]{2,1,0:T(8,128)} %param.14) | data formatting | bytes 8388608 | tf_op args[1]
  236.4 57.4 %all-to-all-done.2 = f32[128,32,256]{2,1,0:T(8,128)} async-done(((f32[128,32,256]{2,1,0:T(8,128)}), f32[128,32,256]{2,1,0:T(8,128)}, u32[]{:S(2)}, u32[]{:S(2)}) %all-to-all-start.2) | async-done | bytes 4194336 | tf_op jit(solution)/shard_map/all_to_all | solution.py:300
  293.8 9.6 %bitcast_multiply_fusion = f32[256,32,128]{0,2,1:T(8,128)} fusion(f32[256,32,128]{0,2,1:T(8,128)} %copy.35, f32[128,32,256]{2,1,0:T(8,128)} %all-to-all-done.2, f32[2,128,128]{2,1,0:T(8,128)S(1)} %copy-done.20, s32[]{:T(128)S(6)} %select_n.51), kind=kOutput, calls=%fused_computation.1 | convolution fusion | flops 806354944 | bytes 12648452 | tf_op jit(solution)/shard_map/cyx,cz->xyz/dot_general | solution.py:301
  303.4 5.4 %copy.36 = f32[256,32,128]{2,1,0:T(8,128)} copy(f32[256,32,128]{0,2,1:T(8,128)} %bitcast_multiply_fusion) | data formatting | bytes 8388608 | tf_op jit(solution)/shard_map/mul | solution.py:302
  (69 shorter events, 20.7 us)
Async XLA Ops:
  10.8 84.3 %all-to-all-start = ((f32[128,32,256]{2,1,0:T(8,128)}), f32[128,32,256]{2,1,0:T(8,128)}, u32[]{:S(2)}, u32[]{:S(2)}) async-start(f32[128,32,256]{2,1,0:T(8,128)} %copy.27), calls=%async_computation | async-start | bytes 8388608 | tf_op jit(solution)/shard_map/all_to_all | solution.py:278
  27.7 63.1 %collective-permute-start.3 = (f32[16,2,8,1024]{3,2,1,0:T(8,128)S(1)}, f32[16,2,8,1024]{3,2,1,0:T(8,128)S(1)}, u32[]{:S(2)}, u32[]{:S(2)}) collective-permute-start(f32[16,2,8,1024]{3,2,1,0:T(8,128)S(1)} %bitcast.48), channel_id=1, source_target_pairs={{0,18},{1,19},{2,0},{3,1},{16,2},{17,3},{18,16},{19,17},{4,22},{5,... | collective-permute-start | bytes 3145736 | tf_op jit(solution)/shard_map/ppermute | solution.py:283
  31.7 60.7 %collective-permute-start.4 = (f32[16,2,8,1024]{3,2,1,0:T(8,128)S(1)}, f32[16,2,8,1024]{3,2,1,0:T(8,128)S(1)}, u32[]{:S(2)}, u32[]{:S(2)}) collective-permute-start(f32[16,2,8,1024]{3,2,1,0:T(8,128)S(1)} %bitcast.47), channel_id=1, source_target_pairs={{0,2},{1,3},{2,16},{3,17},{16,18},{17,19},{18,0},{19,1},{4,6},{5,7... | collective-permute-start | bytes 3145736 | tf_op jit(solution)/shard_map/ppermute | solution.py:284
  95.0 8.0 %copy-start.9 = (bf16[1024,1024]{1,0:T(8,128)(2,1)S(1)}, bf16[1024,1024]{1,0:T(8,128)(2,1)}, u32[]{:S(2)}) copy-start(bf16[1024,1024]{1,0:T(8,128)(2,1)} %constant.96.clone.low) | copy-start | bytes 6291460
  95.0 67.2 %all-to-all-start.1 = ((f32[16,2,2,2,8,1024]{5,4,3,2,1,0:T(8,128)}), f32[16,2,2,2,8,1024]{5,4,3,2,1,0:T(8,128)}, u32[]{:S(2)}, u32[]{:S(2)}) async-start(f32[16,2,2,2,8,1024]{5,4,3,2,1,0:T(8,128)} %pad_maximum_fusion), calls=%async_computation.1 | async-start | bytes 8388608 | tf_op jit(solution)/shard_map/all_to_all | solution.py:286
  103.1 1.6 copy-start.11
  104.7 7.5 %copy-start.10 = (bf16[1024,1024]{1,0:T(8,128)(2,1)S(1)}, bf16[1024,1024]{1,0:T(8,128)(2,1)}, u32[]{:S(2)}) copy-start(bf16[1024,1024]{1,0:T(8,128)(2,1)} %constant.96.clone.low) | copy-start | bytes 6291460
  111.4 14.9 %collective-permute-start.1 = (f32[2,2,128,256]{3,2,1,0:T(8,128)S(1)}, f32[2,2,128,256]{3,2,1,0:T(8,128)S(1)}, u32[]{:S(2)}, u32[]{:S(2)}) collective-permute-start(f32[2,2,128,256]{3,2,1,0:T(8,128)S(1)} %get-tuple-element.23), channel_id=1, source_target_pairs={{0,18},{1,19},{2,0},{3,1},{16,2},{17,3},{18,16},{19,17},{4,22},{5,... | collective-permute-start | bytes 1572872 | tf_op jit(solution)/shard_map/ppermute | solution.py:272
  111.5 22.6 %collective-permute-start.2 = (f32[2,2,128,256]{3,2,1,0:T(8,128)}, f32[2,2,128,256]{3,2,1,0:T(8,128)}, u32[]{:S(2)}, u32[]{:S(2)}) collective-permute-start(f32[2,2,128,256]{3,2,1,0:T(8,128)} %get-tuple-element.24), channel_id=1, source_target_pairs={{0,19},{1,18},{2,1},{3,0},{16,3},{17,2},{18,17},{19,16},{4,23},{5,... | collective-permute-start | bytes 1572872 | tf_op jit(solution)/shard_map/ppermute | solution.py:273
  118.7 15.4 %collective-permute-start = (f32[2,2,128,256]{3,2,1,0:T(8,128)}, f32[2,2,128,256]{3,2,1,0:T(8,128)}, u32[]{:S(2)}, u32[]{:S(2)}) collective-permute-start(f32[2,2,128,256]{3,2,1,0:T(8,128)} %get-tuple-element.22), channel_id=1, source_target_pairs={{0,1},{1,0},{2,3},{3,2},{16,17},{17,16},{18,19},{19,18},{4,5},{5,4... | collective-permute-start | bytes 1572872 | tf_op jit(solution)/shard_map/ppermute | solution.py:271
  119.8 26.1 %collective-permute-start.6 = (f32[2,2,128,256]{3,2,1,0:T(8,128)S(1)}, f32[2,2,128,256]{3,2,1,0:T(8,128)S(1)}, u32[]{:S(2)}, u32[]{:S(2)}) collective-permute-start(f32[2,2,128,256]{3,2,1,0:T(8,128)S(1)} %get-tuple-element.28), channel_id=1, source_target_pairs={{0,1},{1,0},{2,3},{3,2},{16,17},{17,16},{18,19},{19,18},{4,5},{5,4... | collective-permute-start | bytes 1572872 | tf_op jit(solution)/shard_map/ppermute | solution.py:265
  119.8 26.1 %collective-permute-start.7 = (f32[2,2,128,256]{3,2,1,0:T(8,128)S(1)}, f32[2,2,128,256]{3,2,1,0:T(8,128)S(1)}, u32[]{:S(2)}, u32[]{:S(2)}) collective-permute-start(f32[2,2,128,256]{3,2,1,0:T(8,128)S(1)} %get-tuple-element.29), channel_id=1, source_target_pairs={{0,2},{1,3},{2,16},{3,17},{16,18},{17,19},{18,0},{19,1},{4,6},{5,7... | collective-permute-start | bytes 1572872 | tf_op jit(solution)/shard_map/ppermute | solution.py:266
  126.3 20.0 %collective-permute-start.8 = (f32[2,2,128,256]{3,2,1,0:T(8,128)S(1)}, f32[2,2,128,256]{3,2,1,0:T(8,128)}, u32[]{:S(2)}, u32[]{:S(2)}) collective-permute-start(f32[2,2,128,256]{3,2,1,0:T(8,128)S(1)} %get-tuple-element.30), channel_id=1, source_target_pairs={{0,3},{1,2},{2,17},{3,16},{16,19},{17,18},{18,1},{19,0},{4,7},{5,6... | collective-permute-start | bytes 1572872 | tf_op jit(solution)/shard_map/ppermute | solution.py:267
  134.1 1.6 copy-start.7
  135.7 1.6 copy-start.8
  138.4 7.9 %copy-start.17 = (f32[2,2,128,256]{3,2,1,0:T(8,128)S(1)}, f32[2,2,128,256]{3,2,1,0:T(8,128)}, u32[]{:S(2)}) copy-start(f32[2,2,128,256]{3,2,1,0:T(8,128)} %copy-done.16) | copy-start | bytes 1572868
  162.2 1.6 copy-start.3
  163.8 1.6 copy-start.5
  167.0 12.1 %copy-start.4 = (bf16[4,1024,256]{2,1,0:T(8,128)(2,1)S(1)}, bf16[4,1024,256]{2,1,0:T(8,128)(2,1)}, u32[]{:S(2)}) copy-start(bf16[4,1024,256]{2,1,0:T(8,128)(2,1)} %constant.102.clone.low) | copy-start | bytes 6291460
  167.0 12.1 %copy-start.6 = (bf16[4,1024,256]{2,1,0:T(8,128)(2,1)S(1)}, bf16[4,1024,256]{2,1,0:T(8,128)(2,1)}, u32[]{:S(2)}) copy-start(bf16[4,1024,256]{2,1,0:T(8,128)(2,1)} %constant.101.clone.high) | copy-start | bytes 6291460
  167.0 12.1 %copy-start.15 = (f32[2,2,128,1024]{3,2,1,0:T(8,128)S(1)}, f32[2,2,128,1024]{3,2,1,0:T(8,128)}, u32[]{:S(2)}) copy-start(f32[2,2,128,1024]{3,2,1,0:T(8,128)} %copy-done.14) | copy-start | bytes 6291460
  173.9 17.7 %collective-permute-start.12 = (f32[2,2,128,256]{3,2,1,0:T(8,128)S(1)}, f32[2,2,128,256]{3,2,1,0:T(8,128)S(1)}, u32[]{:S(2)}, u32[]{:S(2)}) collective-permute-start(f32[2,2,128,256]{3,2,1,0:T(8,128)S(1)} %get-tuple-element.35), channel_id=1, source_target_pairs={{0,2},{1,3},{2,16},{3,17},{16,18},{17,19},{18,0},{19,1},{4,6},{5,7... | collective-permute-start | bytes 1572872 | tf_op jit(solution)/shard_map/ppermute | solution.py:266
  179.1 21.0 %copy-start.1 = (bf16[1024,1024]{1,0:T(8,128)(2,1)S(1)}, bf16[1024,1024]{1,0:T(8,128)(2,1)}, u32[]{:S(2)}) copy-start(bf16[1024,1024]{1,0:T(8,128)(2,1)} %constant.98.clone.refs_5_) | copy-start | bytes 6291460
  179.1 21.0 %copy-start.2 = (bf16[1024,1024]{1,0:T(8,128)(2,1)S(1)}, bf16[1024,1024]{1,0:T(8,128)(2,1)}, u32[]{:S(2)}) copy-start(bf16[1024,1024]{1,0:T(8,128)(2,1)} %constant.97.clone.refs_4_) | copy-start | bytes 6291460
  179.1 21.0 %collective-permute-start.13 = (f32[2,2,128,256]{3,2,1,0:T(8,128)S(1)}, f32[2,2,128,256]{3,2,1,0:T(8,128)S(1)}, u32[]{:S(2)}, u32[]{:S(2)}) collective-permute-start(f32[2,2,128,256]{3,2,1,0:T(8,128)S(1)} %get-tuple-element.36), channel_id=1, source_target_pairs={{0,3},{1,2},{2,17},{3,16},{16,19},{17,18},{18,1},{19,0},{4,7},{5,6... | collective-permute-start | bytes 1572872 | tf_op jit(solution)/shard_map/ppermute | solution.py:267
  186.1 14.0 %collective-permute-start.11 = (f32[2,2,128,256]{3,2,1,0:T(8,128)S(1)}, f32[2,2,128,256]{3,2,1,0:T(8,128)S(1)}, u32[]{:S(2)}, u32[]{:S(2)}) collective-permute-start(f32[2,2,128,256]{3,2,1,0:T(8,128)S(1)} %get-tuple-element.34), channel_id=1, source_target_pairs={{0,1},{1,0},{2,3},{3,2},{16,17},{17,16},{18,19},{19,18},{4,5},{5,4... | collective-permute-start | bytes 1572872 | tf_op jit(solution)/shard_map/ppermute | solution.py:265
  186.6 18.2 %collective-permute-start.5 = (f32[2,2,128,256]{3,2,1,0:T(8,128)S(1)}, f32[2,2,128,256]{3,2,1,0:T(8,128)S(1)}, u32[]{:S(2)}, u32[]{:S(2)}) collective-permute-start(f32[2,2,128,256]{3,2,1,0:T(8,128)S(1)} %get-tuple-element.26), channel_id=1, source_target_pairs={{0,1},{1,0},{2,3},{3,2},{16,17},{17,16},{18,19},{19,18},{4,5},{5,4... | collective-permute-start | bytes 1572872 | tf_op jit(solution)/shard_map/ppermute | solution.py:271
  186.7 18.1 %collective-permute-start.9 = (f32[2,2,128,256]{3,2,1,0:T(8,128)S(1)}, f32[2,2,128,256]{3,2,1,0:T(8,128)S(1)}, u32[]{:S(2)}, u32[]{:S(2)}) collective-permute-start(f32[2,2,128,256]{3,2,1,0:T(8,128)S(1)} %get-tuple-element.31), channel_id=1, source_target_pairs={{0,18},{1,19},{2,0},{3,1},{16,2},{17,3},{18,16},{19,17},{4,22},{5,... | collective-permute-start | bytes 1572872 | tf_op jit(solution)/shard_map/ppermute | solution.py:272
  191.6 20.7 %collective-permute-start.10 = (f32[2,2,128,256]{3,2,1,0:T(8,128)S(1)}, f32[2,2,128,256]{3,2,1,0:T(8,128)S(1)}, u32[]{:S(2)}, u32[]{:S(2)}) collective-permute-start(f32[2,2,128,256]{3,2,1,0:T(8,128)S(1)} %get-tuple-element.32), channel_id=1, source_target_pairs={{0,19},{1,18},{2,1},{3,0},{16,3},{17,2},{18,17},{19,16},{4,23},{5,... | collective-permute-start | bytes 1572872 | tf_op jit(solution)/shard_map/ppermute | solution.py:273
  216.9 2.0 copy-start
  219.0 74.8 %all-to-all-start.2 = ((f32[128,32,256]{2,1,0:T(8,128)}), f32[128,32,256]{2,1,0:T(8,128)}, u32[]{:S(2)}, u32[]{:S(2)}) async-start(f32[128,32,256]{2,1,0:T(8,128)} %bitcast.44), calls=%async_computation.2 | async-start | bytes 8388608 | tf_op jit(solution)/shard_map/all_to_all | solution.py:300
  231.1 62.7 %copy-start.20 = (f32[2,128,128]{2,1,0:T(8,128)S(1)}, f32[2,128,128]{2,1,0:T(8,128)}, u32[]{:S(2)}) copy-start(f32[2,128,128]{2,1,0:T(8,128)} %constant.93.clone) | copy-start | bytes 393220
  (6 other events, 6.9 us)

commit v2 on v1

v2 whole, which is shorter than its diff:
```python
import functools

import jax
import jax.numpy as jnp
import ml_dtypes
import numpy as np
from jax import lax
from jax.experimental import pallas as pl
from jax.experimental.pallas import tpu as pltpu
from jax.sharding import PartitionSpec as P

F32 = jnp.float32
BF16 = jnp.bfloat16
ALL = ("x", "zh", "y", "zl", "core")
LIMIT = 12 * 1024 * 1024
EDGE_LIMIT = 57 * 1024 * 1024
FAR_LIMIT = 57 * 1024 * 1024
X_LIMIT = 48 * 1024 * 1024


def cosine_table(length):
    freq = np.arange(length, dtype=np.float32)[:, None]
    cells = np.arange(length, dtype=np.float32)[None, :]
    angle = np.float32(np.pi) * (cells + np.float32(0.5)) * freq / np.float32(length)
    scale = np.where(freq == 0, np.sqrt(np.float32(1.0 / length)), np.sqrt(np.float32(2.0 / length)))
    return scale.astype(np.float32) * np.cos(angle.astype(np.float64)).astype(np.float32)


def halves(table):
    high = table.astype(ml_dtypes.bfloat16)
    low = (table - high.astype(np.float32)).astype(ml_dtypes.bfloat16)
    return high, low


def split(value):
    high = value.astype(BF16)
    return high, (value - high.astype(F32)).astype(BF16)


def dot3(a_high, a_low, b_high, b_low):
    dot = functools.partial(jnp.dot, preferred_element_type=F32)
    return dot(a_high, b_high) + dot(a_high, b_low) + dot(a_low, b_high)


def device_id(px, zr, py, core):
    zr = zr % 4
    return (((px * 2 + zr // 2) * 4 + py) * 2 + zr % 2) * 2 + core


def moves(step, flip):
    return [
        (device_id(px, zr, py, core), device_id(px, zr + step, py, core ^ flip))
        for px in range(4)
        for py in range(4)
        for zr in range(4)
        for core in range(2)
    ]


VMEM = pl.BlockSpec(memory_space=pltpu.VMEM)
SMEM = pl.BlockSpec(memory_space=pltpu.SMEM)
PART = jax.ShapeDtypeStruct((2, 2, 128, 256), F32)
RING, X_BLOCKS, B_SETS = 0, 1, (5, 13)


def cost(flops, mib):
    return pl.CostEstimate(flops=int(flops), bytes_accessed=int(mib * 2**20), transcendentals=0)


def z_forward_kernel(_, volume, high, low, out):
    dot = functools.partial(jnp.dot, preferred_element_type=F32)
    for y in range(8):
        v_high, v_low = split(volume[:, y, :].T)
        out[:, y, :] = dot(high[0], v_high) + dot(high[0], v_low) + dot(low[0], v_high)


def z_forward(which, volume, high, low):
    table = pl.BlockSpec((1, 128, 128), lambda y, which: (which[0], 0, 0))
    return pl.pallas_call(
        z_forward_kernel,
        grid_spec=pltpu.PrefetchScalarGridSpec(
            num_scalar_prefetch=1,
            grid=(4,),
            in_specs=[pl.BlockSpec((256, 8, 128), lambda y, which: (0, y, 0)), table, table],
            out_specs=pl.BlockSpec((128, 8, 256), lambda y, which: (0, y, 0)),
        ),
        out_shape=jax.ShapeDtypeStruct((128, 32, 256), F32),
        compiler_params=pltpu.CompilerParams(vmem_limit_bytes=EDGE_LIMIT),
        cost_estimate=cost(3 * 2**28, 8),
        name="z_forward",
    )(which, volume, high, low)


def psf_forward_kernel(_, psf, pick, own, *far):
    dot = functools.partial(jnp.dot, preferred_element_type=F32)
    for b in range(8):
        v_high, v_low = split(psf[:, b, :].T)
        result = dot(pick[0], v_high) + dot(pick[0], v_low)
        result = result.reshape(4, 16, 2, 256)
        for kind in range(2):
            own[:, kind, 0, :, b, :] = result[kind]
            far[kind][:, :, b, :] = result[2 + kind]


def psf_forward(which, psf, pick):
    part = jax.ShapeDtypeStruct((16, 2, 8, 1024), F32)
    whole = jax.ShapeDtypeStruct((16, 2, 2, 2, 8, 1024), F32)
    return pl.pallas_call(
        psf_forward_kernel,
        grid_spec=pltpu.PrefetchScalarGridSpec(
            num_scalar_prefetch=1,
            grid=(4,),
            in_specs=[
                pl.BlockSpec((256, 8, 128), lambda a, which: (a, 0, 0)),
                pl.BlockSpec((1, 128, 128), lambda a, which: (which[0], 0, 0)),
            ],
            out_specs=[pl.BlockSpec((16, 2, 1, 2, 8, 256), lambda a, which: (0, 0, 0, 0, 0, a))]
            + [pl.BlockSpec((16, 2, 8, 256), lambda a, which: (0, 0, 0, a))] * 2,
        ),
        out_shape=[whole, part, part],
        compiler_params=pltpu.CompilerParams(vmem_limit_bytes=EDGE_LIMIT),
        cost_estimate=cost(2**29, 8),
        name="psf_forward",
    )(which, psf, pick)


def z_inverse_kernel(_, volume, estimate, high, low, out):
    dot = functools.partial(jnp.dot, preferred_element_type=F32)
    first = pl.program_id(0) * 8
    for y in range(8):
        v_high, v_low = split(volume[:, first + y, :].T)
        result = dot(v_high, high[0]) + dot(v_low, high[0]) + dot(v_high, low[0])
        out[:, y, :] = result * estimate[:, y, :]


def z_inverse(which, volume, estimate, high, low):
    rows = pl.BlockSpec((256, 8, 128), lambda y, which: (0, y, 0))
    table = pl.BlockSpec((1, 128, 128), lambda y, which: (which[0], 0, 0))
    return pl.pallas_call(
        z_inverse_kernel,
        grid_spec=pltpu.PrefetchScalarGridSpec(
            num_scalar_prefetch=1,
            grid=(4,),
            in_specs=[VMEM, rows, table, table],
            out_specs=rows,
        ),
        out_shape=jax.ShapeDtypeStruct((256, 32, 128), F32),
        compiler_params=pltpu.CompilerParams(vmem_limit_bytes=LIMIT),
        cost_estimate=cost(3 * 2**28, 12),
        name="z_inverse",
    )(which, volume, estimate, high, low)


def y_forward_kernel(slot, places, volume, high, low, *rest):
    outs, rows = rest[:4], rest[4]
    v_high, v_low = split(volume[...].reshape(1024, 256))
    rows[...] = dot3(high[...], low[...], v_high, v_low)
    for part in range(4):
        for q in range(2):
            begin = pl.multiple_of(places[B_SETS[slot] + part * 2 + q] * 128, 128)
            outs[part][q, 0] = rows[pl.ds(begin, 128), :]


def y_forward(places, volume, high, low, slot):
    whole = pl.BlockSpec((1024, 1024), lambda c: (0, 0))
    return pl.pallas_call(
        functools.partial(y_forward_kernel, slot),
        grid=(2,),
        in_specs=[
            SMEM,
            pl.BlockSpec((32, 1, 32, 256), lambda c: (0, 2 * slot + c, 0, 0)),
            whole,
            whole,
        ],
        out_specs=[pl.BlockSpec((2, 1, 128, 256), lambda c: (0, c, 0, 0))] * 4,
        out_shape=[PART] * 4,
        scratch_shapes=[pltpu.VMEM((1024, 256), F32)],
        compiler_params=pltpu.CompilerParams(vmem_limit_bytes=EDGE_LIMIT),
        cost_estimate=cost(3 * 2**30, 8),
        name="y_forward",
    )(places, volume, high, low)


def x_forward_kernel(places, *refs):
    parts, (high, low, out, v_high, v_low) = refs[:4], refs[4:]
    step = pl.program_id(0)

    @pl.when(step == 0)
    def _():
        for k in range(4):
            lanes = pl.ds(pl.multiple_of(places[X_BLOCKS + k] * 256, 256), 256)
            v_high[:, lanes], v_low[:, lanes] = split(parts[k][...].reshape(512, 256))

    total = dot3(v_high[...], v_low[...], high[...], low[...])
    out[...] = total.reshape(2, 2, 128, 256)


def x_forward(places, parts, high, low):
    return pl.pallas_call(
        x_forward_kernel,
        grid=(4,),
        in_specs=[SMEM]
        + [pl.BlockSpec((2, 2, 128, 256), lambda a: (0, 0, 0, 0))] * 4
        + [pl.BlockSpec((1024, 256), lambda a: (0, a))] * 2,
        out_specs=pl.BlockSpec((2, 2, 128, 256), lambda a: (0, 0, 0, a)),
        out_shape=jax.ShapeDtypeStruct((2, 2, 128, 1024), F32),
        scratch_shapes=[pltpu.VMEM((512, 1024), BF16)] * 2,
        compiler_params=pltpu.CompilerParams(vmem_limit_bytes=EDGE_LIMIT),
        cost_estimate=cost(3 * 2**30, 8),
        name="x_forward",
    )(places, *parts, high, low)


def x_inverse_kernel(slot, _, spectrum, psf, high, low, *rest):
    outs, (v_high, v_low) = rest[:4], rest[4:]
    step = pl.program_id(0)

    @pl.when(step == 0)
    def _():
        for q in range(2):
            for c in range(2):
                value = spectrum[q, c] * psf[:, slot, q, c].reshape(128, 1024)
                rows = pl.ds((q * 2 + c) * 128, 128)
                v_high[rows, :], v_low[rows, :] = split(value)

    result = dot3(v_high[...], v_low[...], high[0], low[0]).reshape(2, 2, 128, 256)
    for part in range(4):

        @pl.when(step == part)
        def _():
            outs[part][...] = result


def x_inverse(places, spectrum, psf, high, low, slot):
    table = pl.BlockSpec(
        (1, 1024, 256), lambda step, places: (places[X_BLOCKS + step], 0, 0)
    )
    return pl.pallas_call(
        functools.partial(x_inverse_kernel, slot),
        grid_spec=pltpu.PrefetchScalarGridSpec(
            num_scalar_prefetch=1,
            grid=(4,),
            in_specs=[
                pl.BlockSpec((2, 2, 128, 1024), lambda step, places: (0, 0, 0, 0)),
                VMEM,
                table,
                table,
            ],
            out_specs=[VMEM] * 4,
            scratch_shapes=[pltpu.VMEM((512, 1024), BF16)] * 2,
        ),
        out_shape=[PART] * 4,
        compiler_params=pltpu.CompilerParams(vmem_limit_bytes=X_LIMIT),
        cost_estimate=cost(3 * 2**30, 10),
        name="x_inverse",
    )(places, spectrum, psf, high, low)


def y_inverse_kernel(slot, places, *refs):
    parts, (high, low), (out, v_high, v_low) = refs[:4], refs[4:6], refs[-3:]
    c = pl.program_id(0)
    for part in range(4):
        for q in range(2):
            begin = places[B_SETS[slot] + part * 2 + q] * 128
            rows = pl.ds(pl.multiple_of(begin, 128), 128)
            v_high[rows, :], v_low[rows, :] = split(parts[part][q, c])
    result = dot3(high[...], low[...], v_high[...], v_low[...])
    out[:, 2 * slot + c] = result.reshape(32, 32, 256)


def y_inverse(places, parts, high, low, slot, into):
    args = [places, *parts, high, low] + ([] if into is None else [into])
    return pl.pallas_call(
        functools.partial(y_inverse_kernel, slot),
        grid=(2,),
        in_specs=[SMEM] + [VMEM] * (len(args) - 1),
        out_specs=VMEM,
        out_shape=jax.ShapeDtypeStruct((32, 4, 32, 256), F32),
        scratch_shapes=[pltpu.VMEM((1024, 256), BF16)] * 2,
        input_output_aliases={} if into is None else {7: 0},
        compiler_params=pltpu.CompilerParams(vmem_limit_bytes=LIMIT),
        cost_estimate=cost(3 * 2**30, 8),
        name="y_inverse",
    )(*args)


def local(ratio_field, estimate, psf_spectrum):
    px, zh, py, zl, core = (lax.axis_index(name) for name in ALL)
    ring = 2 * zh + zl
    narrow = 2 * zl + core

    cz = cosine_table(128)
    cz_order = np.array(
        [
            [
                (gx * 4 + gy) * 8 + ((2 * h + low - 1 + side) % 4) * 2 + i
                for gx in range(4)
                for h in range(2)
                for gy in range(4)
                for side in range(2)
                for i in range(2)
            ]
            for low in range(2)
        ]
    )
    z_rows = [jnp.asarray(h) for h in halves(cz[cz_order])]
    pick_order = np.array(
        [
            [
                g * 8 + ((r + shift) % 4) * 2 + i
                for shift in (-1, 0, -2, 1)
                for g in range(16)
                for i in range(2)
            ]
            for r in range(4)
        ]
    )
    pick = jnp.asarray(np.eye(128, dtype=np.float32)[pick_order].astype(ml_dtypes.bfloat16))
    cy = cosine_table(1024)
    b_order = np.array(
        [
            (((gx * 2 + r // 2) * 4 + gy) * 2 + r % 2) * 16 + k * 8 + j
            for r in range(4)
            for k in range(2)
            for gx in range(4)
            for gy in range(4)
            for j in range(8)
        ]
    )
    y_rows = [jnp.asarray(h) for h in halves(cy[b_order])]
    y_columns = [jnp.asarray(h) for h in halves(np.ascontiguousarray(cy[b_order].T))]
    cx = cosine_table(1024)
    x_rows = [jnp.asarray(h) for h in halves(np.ascontiguousarray(cx.T))]
    x_columns = [
        jnp.asarray(h) for h in halves(np.ascontiguousarray(cx.reshape(1024, 4, 256).transpose(1, 0, 2)))
    ]

    partners = ((0, 0), (0, 1), (1, 0), (1, 1))
    places = [ring] + [narrow ^ (2 * far + flip) for far, flip in partners]
    for sign in (-1, 1):
        for far, flip in partners:
            for q in range(2):
                place = ring + sign * (1 + q) if far else ring - sign * q
                places.append((place % 4) * 2 + (core ^ flip))
    places = jnp.stack(places).astype(jnp.int32)

    def send(value, step, flip):
        return lax.ppermute(value, ALL, moves(step, flip))

    def first_all_to_all(value, axes):
        return lax.all_to_all(value, axes, split_axis=0, concat_axis=0, tiled=True)

    def one(value):
        return jnp.asarray(value, jnp.int32).reshape(1)

    def after(value, done):
        return lax.optimization_barrier((value, done))[0]

    volume = z_forward(one(zl), ratio_field, *z_rows)
    volume = first_all_to_all(volume, ("x", "zh", "y")).reshape(32, 4, 32, 256)

    psf, up, down = psf_forward(places, psf_spectrum, pick)
    above, below = send(up, -1, 0), send(down, 1, 0)
    psf, above, below = after((psf, above, below), volume)
    psf = psf.at[:, 0, 1].set(above).at[:, 1, 1].set(below)
    psf = first_all_to_all(psf, ("x", "y"))

    def exchange(lower, upper):
        got_lower = [lower[0], send(lower[1], 0, 1), send(upper[2], 1, 0), send(upper[3], 1, 1)]
        got_upper = [upper[0], send(upper[1], 0, 1), send(lower[2], -1, 0), send(lower[3], -1, 1)]
        return got_lower, got_upper

    lower = y_forward(places, volume, *y_rows, 0)
    upper = y_forward(places, volume, *y_rows, 1)
    lower, upper = exchange(lower, upper)
    lower = x_forward(places, lower, *x_rows)
    upper = x_forward(places, upper, *x_rows)

    lower = x_inverse(places, lower, psf, *x_columns, 0)
    upper = x_inverse(places, upper, psf, *x_columns, 1)
    lower, upper = exchange(lower, upper)
    volume = y_inverse(places, upper, *y_columns, 1, None)
    volume = y_inverse(places, lower, *y_columns, 0, volume)

    volume = first_all_to_all(volume.reshape(128, 32, 256), ("x", "zh", "y"))
    return z_inverse(one(zl), volume, estimate, *z_rows)


def solution(mesh):
    cut = jax.sharding.Mesh(mesh.devices.reshape(4, 2, 4, 2, 2), ALL)
    wide, narrow = ("x", "zh", "y"), ("zl", "core")
    placed = (P(narrow, wide, None), P(narrow, wide, None), P(None, wide + narrow, None))
    return jax.shard_map(
        local, mesh=cut, in_specs=placed, out_specs=P(narrow, wide, None), check_vma=False
    )
```

time: 312 us -> 286 us (0.917)
  blocking collectives: 0 us -> 63.4 us
  waiting for transfers between devices: 157 us -> 105 us
  Pallas kernels: 47 us -> 79.1 us
  local copies, waits for them, and re-layouts: 35.2 us -> 6.47 us
  matrix products: 20.7 us -> 0 us
  starting transfers between devices: 45.4 us -> 30.9 us
    all_to_all x0 -> x1, blocking collectives: none -> 63.4 us  [first_all_to_all(): return lax.all_to_all(value, axes, split_axis=0, concat_axis=0, tiled=True)]
    all_to_all x3 -> x2, waiting for transfers between devices: 66 us -> 3.75 us  [first_all_to_all(): return lax.all_to_all(value, axes, split_axis=0, concat_axis=0, tiled=True)]
    pallas_call x8 -> x11, Pallas kernels: 47 us -> 79.1 us  [the longest x2 16.1 us: x_inverse(): pl.pallas_call(functools.partial(x_inverse_kernel, slot), grid_spec=pltpu...]
    dot_general x3 -> x0, matrix products: 20.7 us -> none  [the longest x1 9.6 us: local(): jnp.einsum('cyx,cz->xyz', volume, table_z, precision=lax.Precision.HIGH)]
    unnamed x43 -> x32, local copies, waits for them, and re-layouts: 22.2 us -> 1.93 us
    all_to_all x3 -> x2, starting transfers between devices: 30.8 us -> 18.8 us  [first_all_to_all(): return lax.all_to_all(value, axes, split_axis=0, concat_axis=0, tiled=True)]
    ppermute x14, waiting for transfers between devices: 91.2 us -> 101 us  [send(): return lax.ppermute(value, ALL, moves(step, flip))]
    mul x1 -> x0, local copies, waits for them, and re-layouts: 5.43 us -> none  [local(): return estimate * volume]
  transfers between devices with their start and end apart: 17 -> 16, of which waited for: 10 -> 7; matrix products, arithmetic and copies ran while one was open for 5% -> 0% of each run, Pallas kernels for 11% -> 18%
where the time goes in v2:
time: 286 us; the launch traced here: 285 us
  waiting for transfers between devices  105 us (37%)
  Pallas kernels  79.1 us (28%)
  blocking collectives  63.4 us (22%)
  starting transfers between devices  30.9 us (11%)
  local copies, waits for them, and re-layouts  6.47 us (2%)
    ppermute x14, waiting for transfers between devices, send(): return lax.ppermute(value, ALL, moves(step, flip))  101 us
    all_to_all x1, blocking collectives, first_all_to_all(): return lax.all_to_all(value, axes, split_axis=0, concat_axis=0, tiled=True)  63.4 us
    all_to_all x2, starting transfers between devices, first_all_to_all(): return lax.all_to_all(value, axes, split_axis=0, concat_axis=0, tiled=True)  18.8 us
    pallas_call x2, Pallas kernels, x_inverse(): pl.pallas_call(functools.partial(x_inverse_kernel, slot), grid_spec=pltpu...  16.1 us
    pallas_call x2, Pallas kernels, x_forward(): pl.pallas_call(x_forward_kernel, grid=(4,), in_specs=[SMEM] + [pl.BlockSp...  15.3 us
    pallas_call x2, Pallas kernels, y_forward(): pl.pallas_call(functools.partial(y_forward_kernel, slot), grid=(2,), in_s...  14.8 us
    ppermute x14, starting transfers between devices, send(): return lax.ppermute(value, ALL, moves(step, flip))  12.2 us
    pallas_call x1, Pallas kernels, z_inverse(): pl.pallas_call(z_inverse_kernel, grid_spec=pltpu.PrefetchScalarGridSpec(n...  9.04 us
  transfers between devices with their start and end apart: 16, of which 7 were waited for; matrix products, arithmetic and copies ran while one was open for 0% of the time, Pallas kernels for 18%

profile of v2, /device:TPU:0, one launch (start us, length us, event | category | flops | bytes accessed | tf_op | source)
XLA Modules:
  0.0 284.9 jit_solution(7813546890467290215)
XLA Ops:
  0.0 7.3 %z_forward.1 = f32[128,32,256]{2,1,0:T(8,128)} custom-call(s32[1]{0:T(128)} %bitcast._, f32[256,32,128]{2,1,0:T(8,128)} %volume.1, bf16[2,128,128]{2,1,0:T(8,128)(2,1)} %constant.150.clone.high, bf16[2,128,128]{2,1,0:T(8,128)(2,1)} %constant.151.clone.low), custom_call_target="tpu_custom_call" | custom-call | flops 805306368 | bytes 8388608 | tf_op jit(solution)/shard_map/z_forward/pallas_call | solution.py:79
  7.3 10.8 %all-to-all-start = ((f32[128,32,256]{2,1,0:T(8,128)}), f32[128,32,256]{2,1,0:T(8,128)}, u32[]{:S(2)}, u32[]{:S(2)}) async-start(f32[128,32,256]{2,1,0:T(8,128)} %z_forward.1), calls=%async_computation | async-start | bytes 8388608 | tf_op jit(solution)/shard_map/all_to_all | solution.py:351
  18.8 7.7 %psf_forward.1 = (f32[16,2,2,2,8,1024]{5,4,3,2,1,0:T(8,128)}, f32[16,2,8,1024]{3,2,1,0:T(8,128)}, f32[16,2,8,1024]{3,2,1,0:T(8,128)}) custom-call(s32[21]{0:T(128)} %stack.69.places._, f32[1024,8,128]{2,1,0:T(8,128)} %psf.1, bf16[4,128,128]{2,1,0:T(8,128)(2,1)} %constant.152.clone.pick), custom_call_target="tpu_custom_call" | custom-call | flops 536870912 | bytes 8388608 | tf_op jit(solution)/shard_map/psf_forward/pallas_call | solution.py:108
  26.5 3.4 %collective-permute-start.3 = (f32[16,2,8,1024]{3,2,1,0:T(8,128)}, f32[16,2,8,1024]{3,2,1,0:T(8,128)S(1)}, u32[]{:S(2)}, u32[]{:S(2)}) collective-permute-start(f32[16,2,8,1024]{3,2,1,0:T(8,128)} %get-tuple-element.56), channel_id=1, source_target_pairs={{0,18},{1,19},{2,0},{3,1},{16,2},{17,3},{18,16},{19,17},{4,22},{5,... | collective-permute-start | bytes 3145736 | tf_op jit(solution)/shard_map/ppermute | solution.py:348
  29.9 0.6 fusion
  30.5 56.8 %collective-permute-done.3 = f32[16,2,8,1024]{3,2,1,0:T(8,128)S(1)} collective-permute-done((f32[16,2,8,1024]{3,2,1,0:T(8,128)}, f32[16,2,8,1024]{3,2,1,0:T(8,128)S(1)}, u32[]{:S(2)}, u32[]{:S(2)}) %collective-permute-start.3) | collective-permute-done | bytes 1048608 | tf_op jit(solution)/shard_map/ppermute | solution.py:348
  87.3 1.8 collective-permute-done.4
  89.1 2.3 bitcast_dynamic-update-slice_fusion.1
  91.4 1.0 bitcast_dynamic-update-slice_fusion
  92.5 7.9 %all-to-all-start.1 = ((f32[16,2,2,2,8,1024]{5,4,3,2,1,0:T(8,128)}), f32[16,2,2,2,8,1024]{5,4,3,2,1,0:T(8,128)}, u32[]{:S(2)}, u32[]{:S(2)}) async-start(f32[16,2,2,2,8,1024]{5,4,3,2,1,0:T(8,128)} %bitcast_dynamic-update-slice_fusion), calls=%async_computation.1 | async-start | bytes 8388608 | tf_op jit(solution)/shard_map/all_to_all | solution.py:351
  100.4 7.4 %y_forward.3 = (f32[2,2,128,256]{3,2,1,0:T(8,128)}, f32[2,2,128,256]{3,2,1,0:T(8,128)}, f32[2,2,128,256]{3,2,1,0:T(8,128)}, f32[2,2,128,256]{3,2,1,0:T(8,128)}) custom-call(s32[21]{0:T(128)} %stack.69.places._, f32[32,4,32,256]{3,2,1,0:T(8,128)} %bitcast.16.volume, bf16[1024,1024]{1,0:T(8,128)(2,1)} %constant.153.clone.high, ...), custom_call_target="tpu_custom_call" | custom-call | flops 3221225472 | bytes 8388608 | tf_op jit(solution)/shard_map/y_forward/pallas_call | solution.py:166
  107.8 7.4 %y_forward.2 = (f32[2,2,128,256]{3,2,1,0:T(8,128)}, f32[2,2,128,256]{3,2,1,0:T(8,128)}, f32[2,2,128,256]{3,2,1,0:T(8,128)}, f32[2,2,128,256]{3,2,1,0:T(8,128)}) custom-call(s32[21]{0:T(128)} %stack.69.places._, f32[32,4,32,256]{3,2,1,0:T(8,128)} %bitcast.16.volume, bf16[1024,1024]{1,0:T(8,128)(2,1)} %constant.153.clone.high, ...), custom_call_target="tpu_custom_call" | custom-call | flops 3221225472 | bytes 8388608 | tf_op jit(solution)/shard_map/y_forward/pallas_call | solution.py:166
  116.2 1.2 collective-permute-start.1
  117.4 1.4 collective-permute-start.2
  119.1 11.1 %collective-permute-done.7.refs_2_ = f32[2,2,128,256]{3,2,1,0:T(8,128)S(1)} collective-permute-done((f32[2,2,128,256]{3,2,1,0:T(8,128)}, f32[2,2,128,256]{3,2,1,0:T(8,128)S(1)}, u32[]{:S(2)}, u32[]{:S(2)}) %collective-permute-start.7) | collective-permute-done | bytes 524320 | tf_op jit(solution)/shard_map/ppermute | solution.py:348
  130.2 10.1 %collective-permute-done.8.refs_3_ = f32[2,2,128,256]{3,2,1,0:T(8,128)S(1)} collective-permute-done((f32[2,2,128,256]{3,2,1,0:T(8,128)}, f32[2,2,128,256]{3,2,1,0:T(8,128)S(1)}, u32[]{:S(2)}, u32[]{:S(2)}) %collective-permute-start.8) | collective-permute-done | bytes 524320 | tf_op jit(solution)/shard_map/ppermute | solution.py:348
  140.4 0.8 copy-done.15
  141.1 7.6 %x_forward.3.spectrum = f32[2,2,128,1024]{3,2,1,0:T(8,128)} custom-call(s32[21]{0:T(128)} %stack.69.places._, f32[2,2,128,256]{3,2,1,0:T(8,128)} %get-tuple-element.63.refs_0_, f32[2,2,128,256]{3,2,1,0:T(8,128)} %copy-done.10, f32[2,2,128,256]{3,2,1,0:T(8,128)} %copy-done.14, f32[2,2,128,256]{3,2,1,0:T(8,128)} %copy-done.15, ...), custom_call_target="tpu_custom_call" | custom-call | flops 3221225472 | bytes 8388608 | tf_op jit(solution)/shard_map/x_forward/pallas_call | solution.py:199
  148.8 0.7 copy-done.11
  149.9 7.7 %x_forward.2.spectrum = f32[2,2,128,1024]{3,2,1,0:T(8,128)} custom-call(s32[21]{0:T(128)} %stack.69.places._, f32[2,2,128,256]{3,2,1,0:T(8,128)} %get-tuple-element.51.refs_0_, f32[2,2,128,256]{3,2,1,0:T(8,128)} %copy-done.13, f32[2,2,128,256]{3,2,1,0:T(8,128)} %copy-done.11, f32[2,2,128,256]{3,2,1,0:T(8,128)} %copy-done.12, ...), custom_call_target="tpu_custom_call" | custom-call | flops 3221225472 | bytes 8388608 | tf_op jit(solution)/shard_map/x_forward/pallas_call | solution.py:199
  157.6 3.7 %all-to-all-done.1.psf = f32[16,2,2,2,8,1024]{5,4,3,2,1,0:T(8,128)} async-done(((f32[16,2,2,2,8,1024]{5,4,3,2,1,0:T(8,128)}), f32[16,2,2,2,8,1024]{5,4,3,2,1,0:T(8,128)}, u32[]{:S(2)}, u32[]{:S(2)}) %all-to-all-start.1) | async-done | bytes 4194336 | tf_op jit(solution)/shard_map/all_to_all | solution.py:351
  161.3 7.9 %x_inverse.3 = (f32[2,2,128,256]{3,2,1,0:T(8,128)S(1)}, f32[2,2,128,256]{3,2,1,0:T(8,128)S(1)}, f32[2,2,128,256]{3,2,1,0:T(8,128)S(1)}, f32[2,2,128,256]{3,2,1,0:T(8,128)S(1)}) custom-call(s32[21]{0:T(128)S(1)} %copy-done.5, f32[2,2,128,1024]{3,2,1,0:T(8,128)S(1)} %copy-done.6, f32[16,2,2,2,8,1024]{5,4,3,2,1,0:T(8,128)} %all-to-all-done.1.psf, ...), custom_call_target="tpu_custom_call" | custom-call | flops 3221225472 | bytes 10485760 | tf_op jit(solution)/shard_map/x_inverse/pallas_call | solution.py:238
  169.4 8.2 %x_inverse.2 = (f32[2,2,128,256]{3,2,1,0:T(8,128)S(1)}, f32[2,2,128,256]{3,2,1,0:T(8,128)S(1)}, f32[2,2,128,256]{3,2,1,0:T(8,128)S(1)}, f32[2,2,128,256]{3,2,1,0:T(8,128)S(1)}) custom-call(s32[21]{0:T(128)S(1)} %copy-done.5, f32[2,2,128,1024]{3,2,1,0:T(8,128)S(1)} %copy-done.7, f32[16,2,2,2,8,1024]{5,4,3,2,1,0:T(8,128)} %all-to-all-done.1.psf, ...), custom_call_target="tpu_custom_call" | custom-call | flops 3221225472 | bytes 10485760 | tf_op jit(solution)/shard_map/x_inverse/pallas_call | solution.py:238
  177.6 1.7 collective-permute-start.13
  179.4 1.0 collective-permute-start.10
  180.4 1.9 collective-permute-start.9
  182.3 10.8 %collective-permute-done.12.refs_2_ = f32[2,2,128,256]{3,2,1,0:T(8,128)S(1)} collective-permute-done((f32[2,2,128,256]{3,2,1,0:T(8,128)S(1)}, f32[2,2,128,256]{3,2,1,0:T(8,128)S(1)}, u32[]{:S(2)}, u32[]{:S(2)}) %collective-permute-start.12) | collective-permute-done | bytes 524320 | tf_op jit(solution)/shard_map/ppermute | solution.py:348
  193.1 10.3 %collective-permute-done.13.refs_3_ = f32[2,2,128,256]{3,2,1,0:T(8,128)S(1)} collective-permute-done((f32[2,2,128,256]{3,2,1,0:T(8,128)S(1)}, f32[2,2,128,256]{3,2,1,0:T(8,128)S(1)}, u32[]{:S(2)}, u32[]{:S(2)}) %collective-permute-start.13) | collective-permute-done | bytes 524320 | tf_op jit(solution)/shard_map/ppermute | solution.py:348
  203.4 4.4 %y_inverse.2.refs_6_ = f32[32,4,32,256]{3,2,1,0:T(8,128)S(1)} custom-call(s32[21]{0:T(128)S(1)} %copy-done.5, f32[2,2,128,256]{3,2,1,0:T(8,128)S(1)} %get-tuple-element.69.refs_0_, f32[2,2,128,256]{3,2,1,0:T(8,128)S(1)} %collective-permute-done.11.refs_1_, f32[2,2,128,256]{3,2,1,0:T(8,128)S(1)} %collective-permute-done.12.refs_2_, ...), custom_call_target="tpu_custom_call" | custom-call | flops 3221225472 | bytes 8388608 | tf_op jit(solution)/shard_map/y_inverse/pallas_call | solution.py:273
  207.9 4.5 %y_inverse.3 = f32[32,4,32,256]{3,2,1,0:T(8,128)S(1)} custom-call(s32[21]{0:T(128)S(1)} %copy-done.5, f32[2,2,128,256]{3,2,1,0:T(8,128)S(1)} %get-tuple-element.61.refs_0_, f32[2,2,128,256]{3,2,1,0:T(8,128)S(1)} %collective-permute-done.5.refs_1_, f32[2,2,128,256]{3,2,1,0:T(8,128)S(1)} %collective-permute-done.9.refs_2_, ...), custom_call_target="tpu_custom_call", output_to_operand_aliasing={{}: (7, {})} | custom-call | flops 3221225472 | bytes 8388608 | tf_op jit(solution)/shard_map/y_inverse/pallas_call | solution.py:273
  212.4 63.4 %all_to_all.15.volume = f32[128,32,256]{2,1,0:T(8,128)S(1)} all-to-all(f32[128,32,256]{2,1,0:T(8,128)S(1)} %bitcast.24), channel_id=1, replica_groups=mesh['x'=4,'zh'=2,'y'=4,'zl'=2,'core'=2] {'x','zh','y'}, dimensions={0} | all-to-all | bytes 8388608 | tf_op jit(solution)/shard_map/all_to_all | solution.py:351
  275.8 9.0 %z_inverse.1 = f32[256,32,128]{2,1,0:T(8,128)} custom-call(s32[1]{0:T(128)} %bitcast._, f32[128,32,256]{2,1,0:T(8,128)S(1)} %all_to_all.15.volume, f32[256,32,128]{2,1,0:T(8,128)S(1)} %copy-done, bf16[2,128,128]{2,1,0:T(8,128)(2,1)S(1)} %copy-done.3, bf16[2,128,128]{2,1,0:T(8,128)(2,1)S(1)} %copy-done.4), custom_call_target="tpu_custom_call" | custom-call | flops 805306368 | bytes 12582912 | tf_op jit(solution)/shard_map/z_inverse/pallas_call | solution.py:139
  (49 shorter events, 2.6 us)
Async XLA Ops:
  7.3 81.9 %all-to-all-start = ((f32[128,32,256]{2,1,0:T(8,128)}), f32[128,32,256]{2,1,0:T(8,128)}, u32[]{:S(2)}, u32[]{:S(2)}) async-start(f32[128,32,256]{2,1,0:T(8,128)} %z_forward.1), calls=%async_computation | async-start | bytes 8388608 | tf_op jit(solution)/shard_map/all_to_all | solution.py:351
  26.5 60.8 %collective-permute-start.3 = (f32[16,2,8,1024]{3,2,1,0:T(8,128)}, f32[16,2,8,1024]{3,2,1,0:T(8,128)S(1)}, u32[]{:S(2)}, u32[]{:S(2)}) collective-permute-start(f32[16,2,8,1024]{3,2,1,0:T(8,128)} %get-tuple-element.56), channel_id=1, source_target_pairs={{0,18},{1,19},{2,0},{3,1},{16,2},{17,3},{18,16},{19,17},{4,22},{5,... | collective-permute-start | bytes 3145736 | tf_op jit(solution)/shard_map/ppermute | solution.py:348
  29.9 59.2 %collective-permute-start.4 = (f32[16,2,8,1024]{3,2,1,0:T(8,128)}, f32[16,2,8,1024]{3,2,1,0:T(8,128)S(1)}, u32[]{:S(2)}, u32[]{:S(2)}) collective-permute-start(f32[16,2,8,1024]{3,2,1,0:T(8,128)} %get-tuple-element.57), channel_id=1, source_target_pairs={{0,2},{1,3},{2,16},{3,17},{16,18},{17,19},{18,0},{19,1},{4,6},{5,7... | collective-permute-start | bytes 3145736 | tf_op jit(solution)/shard_map/ppermute | solution.py:348
  92.5 68.8 %all-to-all-start.1 = ((f32[16,2,2,2,8,1024]{5,4,3,2,1,0:T(8,128)}), f32[16,2,2,2,8,1024]{5,4,3,2,1,0:T(8,128)}, u32[]{:S(2)}, u32[]{:S(2)}) async-start(f32[16,2,2,2,8,1024]{5,4,3,2,1,0:T(8,128)} %bitcast_dynamic-update-slice_fusion), calls=%async_computation.1 | async-start | bytes 8388608 | tf_op jit(solution)/shard_map/all_to_all | solution.py:351
  107.7 8.4 %copy-start.9 = (f32[2,2,128,256]{3,2,1,0:T(8,128)S(1)}, f32[2,2,128,256]{3,2,1,0:T(8,128)}, u32[]{:S(2)}) copy-start(f32[2,2,128,256]{3,2,1,0:T(8,128)} %get-tuple-element.53) | copy-start | bytes 1572868
  107.7 9.6 %copy-start.8 = (f32[2,2,128,256]{3,2,1,0:T(8,128)S(1)}, f32[2,2,128,256]{3,2,1,0:T(8,128)}, u32[]{:S(2)}) copy-start(f32[2,2,128,256]{3,2,1,0:T(8,128)} %get-tuple-element.54) | copy-start | bytes 1572868
  107.8 11.0 %collective-permute-start.6 = (f32[2,2,128,256]{3,2,1,0:T(8,128)}, f32[2,2,128,256]{3,2,1,0:T(8,128)S(1)}, u32[]{:S(2)}, u32[]{:S(2)}) collective-permute-start(f32[2,2,128,256]{3,2,1,0:T(8,128)} %get-tuple-element.64), channel_id=1, source_target_pairs={{0,1},{1,0},{2,3},{3,2},{16,17},{17,16},{18,19},{19,18},{4,5},{5,4... | collective-permute-start | bytes 1572872 | tf_op jit(solution)/shard_map/ppermute | solution.py:348
  115.3 15.0 %collective-permute-start.7 = (f32[2,2,128,256]{3,2,1,0:T(8,128)}, f32[2,2,128,256]{3,2,1,0:T(8,128)S(1)}, u32[]{:S(2)}, u32[]{:S(2)}) collective-permute-start(f32[2,2,128,256]{3,2,1,0:T(8,128)} %get-tuple-element.65), channel_id=1, source_target_pairs={{0,18},{1,19},{2,0},{3,1},{16,2},{17,3},{18,16},{19,17},{4,22},{5,... | collective-permute-start | bytes 1572872 | tf_op jit(solution)/shard_map/ppermute | solution.py:348
  115.6 24.8 %collective-permute-start.8 = (f32[2,2,128,256]{3,2,1,0:T(8,128)}, f32[2,2,128,256]{3,2,1,0:T(8,128)S(1)}, u32[]{:S(2)}, u32[]{:S(2)}) collective-permute-start(f32[2,2,128,256]{3,2,1,0:T(8,128)} %get-tuple-element.66), channel_id=1, source_target_pairs={{0,19},{1,18},{2,1},{3,0},{16,3},{17,2},{18,17},{19,16},{4,23},{5,... | collective-permute-start | bytes 1572872 | tf_op jit(solution)/shard_map/ppermute | solution.py:348
  116.2 32.5 %collective-permute-start.1 = (f32[2,2,128,256]{3,2,1,0:T(8,128)S(1)}, f32[2,2,128,256]{3,2,1,0:T(8,128)S(1)}, u32[]{:S(2)}, u32[]{:S(2)}) collective-permute-start(f32[2,2,128,256]{3,2,1,0:T(8,128)S(1)} %copy-done.9), channel_id=1, source_target_pairs={{0,2},{1,3},{2,16},{3,17},{16,18},{17,19},{18,0},{19,1},{4,6},{5,7... | collective-permute-start | bytes 1572872 | tf_op jit(solution)/shard_map/ppermute | solution.py:348
  117.4 31.4 %collective-permute-start.2 = (f32[2,2,128,256]{3,2,1,0:T(8,128)S(1)}, f32[2,2,128,256]{3,2,1,0:T(8,128)S(1)}, u32[]{:S(2)}, u32[]{:S(2)}) collective-permute-start(f32[2,2,128,256]{3,2,1,0:T(8,128)S(1)} %copy-done.8), channel_id=1, source_target_pairs={{0,3},{1,2},{2,17},{3,16},{16,19},{17,18},{18,1},{19,0},{4,7},{5,6... | collective-permute-start | bytes 1572872 | tf_op jit(solution)/shard_map/ppermute | solution.py:348
  118.8 21.6 %copy-start.10 = (f32[2,2,128,256]{3,2,1,0:T(8,128)}, f32[2,2,128,256]{3,2,1,0:T(8,128)S(1)}, u32[]{:S(2)}) copy-start(f32[2,2,128,256]{3,2,1,0:T(8,128)S(1)} %collective-permute-done.6.refs_1_) | copy-start | bytes 1572868
  118.8 30.0 %collective-permute-start = (f32[2,2,128,256]{3,2,1,0:T(8,128)}, f32[2,2,128,256]{3,2,1,0:T(8,128)S(1)}, u32[]{:S(2)}, u32[]{:S(2)}) collective-permute-start(f32[2,2,128,256]{3,2,1,0:T(8,128)} %get-tuple-element.52), channel_id=1, source_target_pairs={{0,1},{1,0},{2,3},{3,2},{16,17},{17,16},{18,19},{19,18},{4,5},{5,4... | collective-permute-start | bytes 1572872 | tf_op jit(solution)/shard_map/ppermute | solution.py:348
  130.2 10.1 %copy-start.14 = (f32[2,2,128,256]{3,2,1,0:T(8,128)}, f32[2,2,128,256]{3,2,1,0:T(8,128)S(1)}, u32[]{:S(2)}) copy-start(f32[2,2,128,256]{3,2,1,0:T(8,128)S(1)} %collective-permute-done.7.refs_2_) | copy-start | bytes 1572868
  140.3 0.8 copy-start.15
  148.7 0.8 copy-start.11
  148.7 1.0 copy-start.12
  148.8 1.1 copy-start.13
  149.9 11.5 %copy-start.5 = (s32[21]{0:T(128)S(1)}, s32[21]{0:T(128)}, u32[]{:S(2)}) copy-start(s32[21]{0:T(128)} %stack.69.places._) | copy-start | bytes 256
  149.9 11.5 %copy-start.6 = (f32[2,2,128,1024]{3,2,1,0:T(8,128)S(1)}, f32[2,2,128,1024]{3,2,1,0:T(8,128)}, u32[]{:S(2)}) copy-start(f32[2,2,128,1024]{3,2,1,0:T(8,128)} %x_forward.3.spectrum) | copy-start | bytes 6291460
  161.3 8.0 %copy-start.7 = (f32[2,2,128,1024]{3,2,1,0:T(8,128)S(1)}, f32[2,2,128,1024]{3,2,1,0:T(8,128)}, u32[]{:S(2)}) copy-start(f32[2,2,128,1024]{3,2,1,0:T(8,128)} %x_forward.2.spectrum) | copy-start | bytes 6291460
  169.2 34.2 %copy-start.1 = (bf16[1024,1024]{1,0:T(8,128)(2,1)S(1)}, bf16[1024,1024]{1,0:T(8,128)(2,1)}, u32[]{:S(2)}) copy-start(bf16[1024,1024]{1,0:T(8,128)(2,1)} %constant.155.clone.refs_4_) | copy-start | bytes 6291460
  169.3 34.2 %copy-start.2 = (bf16[1024,1024]{1,0:T(8,128)(2,1)S(1)}, bf16[1024,1024]{1,0:T(8,128)(2,1)}, u32[]{:S(2)}) copy-start(bf16[1024,1024]{1,0:T(8,128)(2,1)} %constant.156.clone.refs_5_) | copy-start | bytes 6291460
  169.3 13.0 %collective-permute-start.11 = (f32[2,2,128,256]{3,2,1,0:T(8,128)S(1)}, f32[2,2,128,256]{3,2,1,0:T(8,128)S(1)}, u32[]{:S(2)}, u32[]{:S(2)}) collective-permute-start(f32[2,2,128,256]{3,2,1,0:T(8,128)S(1)} %get-tuple-element.70), channel_id=1, source_target_pairs={{0,1},{1,0},{2,3},{3,2},{16,17},{17,16},{18,19},{19,18},{4,5},{5,4... | collective-permute-start | bytes 1572872 | tf_op jit(solution)/shard_map/ppermute | solution.py:348
  177.5 15.6 %collective-permute-start.12 = (f32[2,2,128,256]{3,2,1,0:T(8,128)S(1)}, f32[2,2,128,256]{3,2,1,0:T(8,128)S(1)}, u32[]{:S(2)}, u32[]{:S(2)}) collective-permute-start(f32[2,2,128,256]{3,2,1,0:T(8,128)S(1)} %get-tuple-element.71), channel_id=1, source_target_pairs={{0,18},{1,19},{2,0},{3,1},{16,2},{17,3},{18,16},{19,17},{4,22},{5,... | collective-permute-start | bytes 1572872 | tf_op jit(solution)/shard_map/ppermute | solution.py:348
  177.6 25.8 %collective-permute-start.13 = (f32[2,2,128,256]{3,2,1,0:T(8,128)S(1)}, f32[2,2,128,256]{3,2,1,0:T(8,128)S(1)}, u32[]{:S(2)}, u32[]{:S(2)}) collective-permute-start(f32[2,2,128,256]{3,2,1,0:T(8,128)S(1)} %get-tuple-element.72), channel_id=1, source_target_pairs={{0,19},{1,18},{2,1},{3,0},{16,3},{17,2},{18,17},{19,16},{4,23},{5,... | collective-permute-start | bytes 1572872 | tf_op jit(solution)/shard_map/ppermute | solution.py:348
  179.4 28.5 %collective-permute-start.10 = (f32[2,2,128,256]{3,2,1,0:T(8,128)S(1)}, f32[2,2,128,256]{3,2,1,0:T(8,128)S(1)}, u32[]{:S(2)}, u32[]{:S(2)}) collective-permute-start(f32[2,2,128,256]{3,2,1,0:T(8,128)S(1)} %get-tuple-element.68), channel_id=1, source_target_pairs={{0,3},{1,2},{2,17},{3,16},{16,19},{17,18},{18,1},{19,0},{4,7},{5,6... | collective-permute-start | bytes 1572872 | tf_op jit(solution)/shard_map/ppermute | solution.py:348
  180.4 27.5 %collective-permute-start.9 = (f32[2,2,128,256]{3,2,1,0:T(8,128)S(1)}, f32[2,2,128,256]{3,2,1,0:T(8,128)S(1)}, u32[]{:S(2)}, u32[]{:S(2)}) collective-permute-start(f32[2,2,128,256]{3,2,1,0:T(8,128)S(1)} %get-tuple-element.67), channel_id=1, source_target_pairs={{0,2},{1,3},{2,16},{3,17},{16,18},{17,19},{18,0},{19,1},{4,6},{5,7... | collective-permute-start | bytes 1572872 | tf_op jit(solution)/shard_map/ppermute | solution.py:348
  182.3 25.7 %collective-permute-start.5 = (f32[2,2,128,256]{3,2,1,0:T(8,128)S(1)}, f32[2,2,128,256]{3,2,1,0:T(8,128)S(1)}, u32[]{:S(2)}, u32[]{:S(2)}) collective-permute-start(f32[2,2,128,256]{3,2,1,0:T(8,128)S(1)} %get-tuple-element.62), channel_id=1, source_target_pairs={{0,1},{1,0},{2,3},{3,2},{16,17},{17,16},{18,19},{19,18},{4,5},{5,4... | collective-permute-start | bytes 1572872 | tf_op jit(solution)/shard_map/ppermute | solution.py:348
  212.4 63.5 %copy-start = (f32[256,32,128]{2,1,0:T(8,128)S(1)}, f32[256,32,128]{2,1,0:T(8,128)}, u32[]{:S(2)}) copy-start(f32[256,32,128]{2,1,0:T(8,128)} %estimate.1) | copy-start | bytes 12582916
  212.4 63.4 %copy-start.3 = (bf16[2,128,128]{2,1,0:T(8,128)(2,1)S(1)}, bf16[2,128,128]{2,1,0:T(8,128)(2,1)}, u32[]{:S(2)}) copy-start(bf16[2,128,128]{2,1,0:T(8,128)(2,1)} %constant.150.clone.high) | copy-start | bytes 196612
  212.4 63.4 %copy-start.4 = (bf16[2,128,128]{2,1,0:T(8,128)(2,1)S(1)}, bf16[2,128,128]{2,1,0:T(8,128)(2,1)}, u32[]{:S(2)}) copy-start(bf16[2,128,128]{2,1,0:T(8,128)(2,1)} %constant.151.clone.low) | copy-start | bytes 196612

commit v3 on v2

--- a/solution.py
+++ b/solution.py
@@ -15,7 +15,7 @@
 LIMIT = 12 * 1024 * 1024
 EDGE_LIMIT = 57 * 1024 * 1024
 FAR_LIMIT = 57 * 1024 * 1024
-X_LIMIT = 48 * 1024 * 1024
+X_LIMIT = 50 * 1024 * 1024
 
 
 def cosine_table(length):
@@ -60,7 +60,8 @@
 VMEM = pl.BlockSpec(memory_space=pltpu.VMEM)
 SMEM = pl.BlockSpec(memory_space=pltpu.SMEM)
 PART = jax.ShapeDtypeStruct((2, 2, 128, 256), F32)
-RING, X_BLOCKS, B_SETS = 0, 1, (5, 13)
+RING, X_BLOCKS, B_SETS = 0, 1, 5
+BOTH = jax.ShapeDtypeStruct((2, 2, 2, 128, 256), F32)
 
 
 def cost(flops, mib):
@@ -91,20 +92,19 @@
     )(which, volume, high, low)
 
 
-def psf_forward_kernel(_, psf, pick, own, *far):
+def psf_forward_kernel(_, psf, pick, own, far):
     dot = functools.partial(jnp.dot, preferred_element_type=F32)
     for b in range(8):
         v_high, v_low = split(psf[:, b, :].T)
         result = dot(pick[0], v_high) + dot(pick[0], v_low)
         result = result.reshape(4, 16, 2, 256)
         for kind in range(2):
-            own[:, kind, 0, :, b, :] = result[kind]
-            far[kind][:, :, b, :] = result[2 + kind]
+            own[:, kind, :, b, :] = result[kind]
+            far[:, kind, :, b, :] = result[2 + kind]
 
 
 def psf_forward(which, psf, pick):
-    part = jax.ShapeDtypeStruct((16, 2, 8, 1024), F32)
-    whole = jax.ShapeDtypeStruct((16, 2, 2, 2, 8, 1024), F32)
+    near = jax.ShapeDtypeStruct((16, 2, 2, 8, 1024), F32)
     return pl.pallas_call(
         psf_forward_kernel,
         grid_spec=pltpu.PrefetchScalarGridSpec(
@@ -114,10 +114,9 @@
                 pl.BlockSpec((256, 8, 128), lambda a, which: (a, 0, 0)),
                 pl.BlockSpec((1, 128, 128), lambda a, which: (which[0], 0, 0)),
             ],
-            out_specs=[pl.BlockSpec((16, 2, 1, 2, 8, 256), lambda a, which: (0, 0, 0, 0, 0, a))]
-            + [pl.BlockSpec((16, 2, 8, 256), lambda a, which: (0, 0, 0, a))] * 2,
+            out_specs=[pl.BlockSpec((16, 2, 2, 8, 256), lambda a, which: (0, 0, 0, 0, a))] * 2,
         ),
-        out_shape=[whole, part, part],
+        out_shape=[near, near],
         compiler_params=pltpu.CompilerParams(vmem_limit_bytes=EDGE_LIMIT),
         cost_estimate=cost(2**29, 8),
         name="psf_forward",
@@ -151,137 +150,168 @@
     )(which, volume, estimate, high, low)
 
 
-def y_forward_kernel(slot, places, volume, high, low, *rest):
-    outs, rows = rest[:4], rest[4]
+def y_forward_kernel(places, volume, high, low, own, across, *rest):
+    along, rows = rest[:4], rest[4]
+    slot = pl.program_id(0) // 2
     v_high, v_low = split(volume[...].reshape(1024, 256))
     rows[...] = dot3(high[...], low[...], v_high, v_low)
-    for part in range(4):
-        for q in range(2):
-            begin = pl.multiple_of(places[B_SETS[slot] + part * 2 + q] * 128, 128)
-            outs[part][q, 0] = rows[pl.ds(begin, 128), :]
-
-
-def y_forward(places, volume, high, low, slot):
+
+    def block(part, q):
+        begin = places[B_SETS + slot * 8 + part * 2 + q] * 128
+        return rows[pl.ds(pl.multiple_of(begin, 128), 128), :]
+
+    for q in range(2):
+        own[0, q, 0] = block(0, q)
+        across[0, q, 0] = block(1, q)
+        for side in range(2):
+
+            @pl.when(slot == side)
+            def _():
+                along[2 * side][q, 0] = block(2, q)
+                along[2 * side + 1][q, 0] = block(3, q)
+
+
+def y_forward(places, volume, high, low):
     whole = pl.BlockSpec((1024, 1024), lambda c: (0, 0))
-    return pl.pallas_call(
-        functools.partial(y_forward_kernel, slot),
-        grid=(2,),
-        in_specs=[
-            SMEM,
-            pl.BlockSpec((32, 1, 32, 256), lambda c: (0, 2 * slot + c, 0, 0)),
-            whole,
-            whole,
-        ],
-        out_specs=[pl.BlockSpec((2, 1, 128, 256), lambda c: (0, c, 0, 0))] * 4,
-        out_shape=[PART] * 4,
+    both = pl.BlockSpec((1, 2, 1, 128, 256), lambda c: (c // 2, 0, c % 2, 0, 0))
+    down = pl.BlockSpec((2, 1, 128, 256), lambda c: (0, jnp.minimum(c, 1), 0, 0))
+    up = pl.BlockSpec((2, 1, 128, 256), lambda c: (0, jnp.maximum(c - 2, 0), 0, 0))
+    return pl.pallas_call(
+        y_forward_kernel,
+        grid=(4,),
+        in_specs=[SMEM, pl.BlockSpec((32, 1, 32, 256), lambda c: (0, c, 0, 0)), whole, whole],
+        out_specs=[both, both, down, down, up, up],
+        out_shape=[BOTH, BOTH] + [PART] * 4,
         scratch_shapes=[pltpu.VMEM((1024, 256), F32)],
         compiler_params=pltpu.CompilerParams(vmem_limit_bytes=EDGE_LIMIT),
-        cost_estimate=cost(3 * 2**30, 8),
+        cost_estimate=cost(6 * 2**30, 12),
         name="y_forward",
     )(places, volume, high, low)
 
 
-def x_forward_kernel(places, *refs):
-    parts, (high, low, out, v_high, v_low) = refs[:4], refs[4:]
+def x_forward_kernel(places, own, across, *refs):
+    along, (high, low, out, v_high, v_low) = refs[:4], refs[4:]
     step = pl.program_id(0)
 
     @pl.when(step == 0)
     def _():
-        for k in range(4):
-            lanes = pl.ds(pl.multiple_of(places[X_BLOCKS + k] * 256, 256), 256)
-            v_high[:, lanes], v_low[:, lanes] = split(parts[k][...].reshape(512, 256))
+        for slot in range(2):
+            for k in range(4):
+                part = (own, across)[k].at[slot] if k < 2 else along[2 * slot + k - 2]
+                rows = pl.ds(slot * 512, 512)
+                lanes = pl.ds(pl.multiple_of(places[X_BLOCKS + k] * 256, 256), 256)
+                v_high[rows, lanes], v_low[rows, lanes] = split(part[...].reshape(512, 256))
 
     total = dot3(v_high[...], v_low[...], high[...], low[...])
-    out[...] = total.reshape(2, 2, 128, 256)
-
-
-def x_forward(places, parts, high, low):
+    out[...] = total.reshape(2, 2, 2, 128, 256)
+
+
+def x_forward(places, own, across, along, high, low):
     return pl.pallas_call(
         x_forward_kernel,
         grid=(4,),
         in_specs=[SMEM]
+        + [pl.BlockSpec((2, 2, 2, 128, 256), lambda a: (0, 0, 0, 0, 0))] * 2
         + [pl.BlockSpec((2, 2, 128, 256), lambda a: (0, 0, 0, 0))] * 4
         + [pl.BlockSpec((1024, 256), lambda a: (0, a))] * 2,
-        out_specs=pl.BlockSpec((2, 2, 128, 256), lambda a: (0, 0, 0, a)),
-        out_shape=jax.ShapeDtypeStruct((2, 2, 128, 1024), F32),
-        scratch_shapes=[pltpu.VMEM((512, 1024), BF16)] * 2,
+        out_specs=pl.BlockSpec((2, 2, 2, 128, 256), lambda a: (0, 0, 0, 0, a)),
+        out_shape=jax.ShapeDtypeStruct((2, 2, 2, 128, 1024), F32),
+        scratch_shapes=[pltpu.VMEM((1024, 1024), BF16)] * 2,
         compiler_params=pltpu.CompilerParams(vmem_limit_bytes=EDGE_LIMIT),
-        cost_estimate=cost(3 * 2**30, 8),
+        cost_estimate=cost(6 * 2**30, 12),
         name="x_forward",
-    )(places, *parts, high, low)
-
-
-def x_inverse_kernel(slot, _, spectrum, psf, high, low, *rest):
-    outs, (v_high, v_low) = rest[:4], rest[4:]
+    )(places, own, across, *along, high, low)
+
+
+def x_inverse_kernel(_, spectrum, near, above, below, high, low, own, across, *rest):
+    along, (v_high, v_low) = rest[:4], rest[4:]
     step = pl.program_id(0)
 
     @pl.when(step == 0)
     def _():
-        for q in range(2):
-            for c in range(2):
-                value = spectrum[q, c] * psf[:, slot, q, c].reshape(128, 1024)
-                rows = pl.ds((q * 2 + c) * 128, 128)
-                v_high[rows, :], v_low[rows, :] = split(value)
-
-    result = dot3(v_high[...], v_low[...], high[0], low[0]).reshape(2, 2, 128, 256)
-    for part in range(4):
-
-        @pl.when(step == part)
+        for slot in range(2):
+            for q in range(2):
+                for c in range(2):
+                    psf = (above, below)[slot][:, c] if q else near[:, slot, c]
+                    value = spectrum[slot, q, c] * psf.reshape(128, 1024)
+                    rows = pl.ds(slot * 512 + q * 256 + c * 128, 128)
+                    v_high[rows, :], v_low[rows, :] = split(value)
+
+    result = dot3(v_high[...], v_low[...], high[0], low[0]).reshape(2, 2, 2, 128, 256)
+    for k in range(2):
+
+        @pl.when(step == k)
         def _():
-            outs[part][...] = result
-
-
-def x_inverse(places, spectrum, psf, high, low, slot):
-    table = pl.BlockSpec(
-        (1, 1024, 256), lambda step, places: (places[X_BLOCKS + step], 0, 0)
-    )
-    return pl.pallas_call(
-        functools.partial(x_inverse_kernel, slot),
+            along[k][...] = result[0]
+            along[2 + k][...] = result[1]
+
+    @pl.when(step == 2)
+    def _():
+        across[...] = result
+
+    @pl.when(step == 3)
+    def _():
+        own[...] = result
+
+
+def x_inverse(places, spectrum, near, above, below, high, low):
+    def block(step, places):
+        return places[X_BLOCKS + jnp.where(step < 2, step + 2, 3 - step)], 0, 0
+
+    table = pl.BlockSpec((1, 1024, 256), block)
+    whole = pl.BlockSpec((2, 2, 2, 128, 1024), lambda step, places: (0, 0, 0, 0, 0))
+    far = pl.BlockSpec((16, 2, 8, 1024), lambda step, places: (0, 0, 0, 0))
+    return pl.pallas_call(
+        x_inverse_kernel,
         grid_spec=pltpu.PrefetchScalarGridSpec(
             num_scalar_prefetch=1,
             grid=(4,),
-            in_specs=[
-                pl.BlockSpec((2, 2, 128, 1024), lambda step, places: (0, 0, 0, 0)),
-                VMEM,
-                table,
-                table,
-            ],
-            out_specs=[VMEM] * 4,
-            scratch_shapes=[pltpu.VMEM((512, 1024), BF16)] * 2,
+            in_specs=[whole, VMEM, far, far, table, table],
+            out_specs=[VMEM] * 6,
+            scratch_shapes=[pltpu.VMEM((1024, 1024), BF16)] * 2,
         ),
-        out_shape=[PART] * 4,
+        out_shape=[BOTH, BOTH] + [PART] * 4,
         compiler_params=pltpu.CompilerParams(vmem_limit_bytes=X_LIMIT),
-        cost_estimate=cost(3 * 2**30, 10),
+        cost_estimate=cost(6 * 2**30, 16),
         name="x_inverse",
-    )(places, spectrum, psf, high, low)
-
-
-def y_inverse_kernel(slot, places, *refs):
-    parts, (high, low), (out, v_high, v_low) = refs[:4], refs[4:6], refs[-3:]
-    c = pl.program_id(0)
-    for part in range(4):
-        for q in range(2):
-            begin = places[B_SETS[slot] + part * 2 + q] * 128
-            rows = pl.ds(pl.multiple_of(begin, 128), 128)
-            v_high[rows, :], v_low[rows, :] = split(parts[part][q, c])
+    )(places, spectrum, near, above, below, high, low)
+
+
+def y_inverse_kernel(places, own, across, *refs):
+    along, (high, low, out, v_high, v_low) = refs[:4], refs[4:]
+    slot, c = pl.program_id(0) // 2, pl.program_id(0) % 2
+
+    def place(part, q, value):
+        begin = places[B_SETS + slot * 8 + part * 2 + q] * 128
+        rows = pl.ds(pl.multiple_of(begin, 128), 128)
+        v_high[rows, :], v_low[rows, :] = split(value)
+
+    for q in range(2):
+        place(0, q, own[slot, q, c])
+        place(1, q, across[slot, q, c])
+        for side in range(2):
+
+            @pl.when(slot == side)
+            def _():
+                place(2, q, along[2 * side][q, c])
+                place(3, q, along[2 * side + 1][q, c])
+
     result = dot3(high[...], low[...], v_high[...], v_low[...])
     out[:, 2 * slot + c] = result.reshape(32, 32, 256)
 
 
-def y_inverse(places, parts, high, low, slot, into):
-    args = [places, *parts, high, low] + ([] if into is None else [into])
-    return pl.pallas_call(
-        functools.partial(y_inverse_kernel, slot),
-        grid=(2,),
-        in_specs=[SMEM] + [VMEM] * (len(args) - 1),
+def y_inverse(places, own, across, along, high, low):
+    return pl.pallas_call(
+        y_inverse_kernel,
+        grid=(4,),
+        in_specs=[SMEM] + [VMEM] * 8,
         out_specs=VMEM,
         out_shape=jax.ShapeDtypeStruct((32, 4, 32, 256), F32),
         scratch_shapes=[pltpu.VMEM((1024, 256), BF16)] * 2,
-        input_output_aliases={} if into is None else {7: 0},
         compiler_params=pltpu.CompilerParams(vmem_limit_bytes=LIMIT),
-        cost_estimate=cost(3 * 2**30, 8),
+        cost_estimate=cost(6 * 2**30, 12),
         name="y_inverse",
-    )(*args)
+    )(places, own, across, *along, high, low)
 
 
 def local(ratio_field, estimate, psf_spectrum):
@@ -359,28 +389,20 @@
     volume = z_forward(one(zl), ratio_field, *z_rows)
     volume = first_all_to_all(volume, ("x", "zh", "y")).reshape(32, 4, 32, 256)
 
-    psf, up, down = psf_forward(places, psf_spectrum, pick)
-    above, below = send(up, -1, 0), send(down, 1, 0)
-    psf, above, below = after((psf, above, below), volume)
-    psf = psf.at[:, 0, 1].set(above).at[:, 1, 1].set(below)
-    psf = first_all_to_all(psf, ("x", "y"))
-
-    def exchange(lower, upper):
-        got_lower = [lower[0], send(lower[1], 0, 1), send(upper[2], 1, 0), send(upper[3], 1, 1)]
-        got_upper = [upper[0], send(upper[1], 0, 1), send(lower[2], -1, 0), send(lower[3], -1, 1)]
-        return got_lower, got_upper
-
-    lower = y_forward(places, volume, *y_rows, 0)
-    upper = y_forward(places, volume, *y_rows, 1)
-    lower, upper = exchange(lower, upper)
-    lower = x_forward(places, lower, *x_rows)
-    upper = x_forward(places, upper, *x_rows)
-
-    lower = x_inverse(places, lower, psf, *x_columns, 0)
-    upper = x_inverse(places, upper, psf, *x_columns, 1)
-    lower, upper = exchange(lower, upper)
-    volume = y_inverse(places, upper, *y_columns, 1, None)
-    volume = y_inverse(places, lower, *y_columns, 0, volume)
+    near, far = psf_forward(places, psf_spectrum, pick)
+    far = first_all_to_all(after(far, volume), ("x", "y"))
+
+    def exchange(own, across, *along):
+        from_above = [send(along[0], -1, 0), send(along[1], -1, 1)]
+        from_below = [send(along[2], 1, 0), send(along[3], 1, 1)]
+        return own, send(across, 0, 1), from_below + from_above
+
+    parts = exchange(*y_forward(places, volume, *y_rows))
+    near = first_all_to_all(after(near, (far, parts[2][0], parts[2][2])), ("x", "y"))
+    above, below = send(far[:, 0], -1, 0), send(far[:, 1], 1, 0)
+    spectrum = x_forward(places, *parts, *x_rows)
+    parts = exchange(*x_inverse(places, spectrum, near, above, below, *x_columns))
+    volume = y_inverse(places, *parts, *y_columns)
 
     volume = first_all_to_all(volume.reshape(128, 32, 256), ("x", "zh", "y"))
     return z_inverse(one(zl), volume, estimate, *z_rows)

time: 286 us -> 280 us (0.979)
  Pallas kernels: 79.1 us -> 69.4 us
  starting transfers between devices: 30.9 us -> 36.1 us
  blocking collectives: 63.4 us -> 59.4 us
  waiting for transfers between devices: 105 us -> 108 us
    all_to_all x2 -> x3, waiting for transfers between devices: 3.75 us -> 54.8 us  [first_all_to_all(): return lax.all_to_all(value, axes, split_axis=0, concat_axis=0, tiled=True)]
    ppermute x14 -> x12, waiting for transfers between devices: 101 us -> 53.7 us  [send(): return lax.ppermute(value, ALL, moves(step, flip))]
    pallas_call x6 -> x3, Pallas kernels: 39.7 us -> 33.7 us  [the longest x1 13.7 us: x_inverse(): pl.pallas_call(x_inverse_kernel, grid_spec=pltpu.PrefetchScalarGridSpec(n...]
    all_to_all x1, blocking collectives: 63.4 us -> 59.4 us  [first_all_to_all(): return lax.all_to_all(value, axes, split_axis=0, concat_axis=0, tiled=True)]
    pallas_call x2 -> x1, Pallas kernels: 15.3 us -> 11.6 us  [x_forward(): pl.pallas_call(x_forward_kernel, grid=(4,), in_specs=[SMEM] + [pl.BlockSp...]
    scatter x2 -> x0, local copies, waits for them, and re-layouts: 3.35 us -> none  [local(): psf = psf.at[:, 0, 1].set(above).at[:, 1, 1].set(below)]
    all_to_all x2 -> x3, starting transfers between devices: 18.8 us -> 21.6 us  [first_all_to_all(): return lax.all_to_all(value, axes, split_axis=0, concat_axis=0, tiled=True)]
    ppermute x14 -> x12, starting transfers between devices: 12.2 us -> 14.5 us  [send(): return lax.ppermute(value, ALL, moves(step, flip))]
  transfers between devices with their start and end apart: 16 -> 15, of which waited for: 7 -> 9; matrix products, arithmetic and copies ran while one was open for 0% -> 0% of each run, Pallas kernels for 18% -> 11%
where the time goes in v3:
time: 280 us; the launch traced here: 278 us
  waiting for transfers between devices  108 us (39%)
  Pallas kernels  69.4 us (25%)
  blocking collectives  59.4 us (21%)
  starting transfers between devices  36.1 us (13%)
  local copies, waits for them, and re-layouts  4.53 us (2%)
    all_to_all x1, blocking collectives, first_all_to_all(): return lax.all_to_all(value, axes, split_axis=0, concat_axis=0, tiled=True)  59.4 us
    all_to_all x3, waiting for transfers between devices, first_all_to_all(): return lax.all_to_all(value, axes, split_axis=0, concat_axis=0, tiled=True)  54.8 us
    ppermute x12, waiting for transfers between devices, send(): return lax.ppermute(value, ALL, moves(step, flip))  53.7 us
    all_to_all x3, starting transfers between devices, first_all_to_all(): return lax.all_to_all(value, axes, split_axis=0, concat_axis=0, tiled=True)  21.6 us
    ppermute x12, starting transfers between devices, send(): return lax.ppermute(value, ALL, moves(step, flip))  14.5 us
    pallas_call x1, Pallas kernels, x_inverse(): pl.pallas_call(x_inverse_kernel, grid_spec=pltpu.PrefetchScalarGridSpec(n...  13.7 us
    pallas_call x1, Pallas kernels, y_forward(): pl.pallas_call(y_forward_kernel, grid=(4,), in_specs=[SMEM, pl.BlockSpec(...  11.7 us
    pallas_call x1, Pallas kernels, x_forward(): pl.pallas_call(x_forward_kernel, grid=(4,), in_specs=[SMEM] + [pl.BlockSp...  11.6 us
  transfers between devices with their start and end apart: 15, of which 9 were waited for; matrix products, arithmetic and copies ran while one was open for 0% of the time, Pallas kernels for 11%

profile of v3, /device:TPU:0, one launch (start us, length us, event | category | flops | bytes accessed | tf_op | source)
XLA Modules:
  0.0 278.1 jit_solution(10873231504952703118)
XLA Ops:
  0.0 7.3 %z_forward.1 = f32[128,32,256]{2,1,0:T(8,128)} custom-call(s32[1]{0:T(128)} %bitcast._, f32[256,32,128]{2,1,0:T(8,128)} %volume.1, bf16[2,128,128]{2,1,0:T(8,128)(2,1)} %constant.94.clone.high, bf16[2,128,128]{2,1,0:T(8,128)(2,1)} %constant.95.clone.low), custom_call_target="tpu_custom_call" | custom-call | flops 805306368 | bytes 8388608 | tf_op jit(solution)/shard_map/z_forward/pallas_call | solution.py:80
  7.3 10.8 %all-to-all-start = ((f32[128,32,256]{2,1,0:T(8,128)}), f32[128,32,256]{2,1,0:T(8,128)}, u32[]{:S(2)}, u32[]{:S(2)}) async-start(f32[128,32,256]{2,1,0:T(8,128)} %z_forward.1), calls=%async_computation | async-start | bytes 8388608 | tf_op jit(solution)/shard_map/all_to_all | solution.py:381
  18.2 0.7 stack.69.places._
  18.8 7.7 %psf_forward.1 = (f32[16,2,2,8,1024]{4,3,2,1,0:T(8,128)}, f32[16,2,2,8,1024]{4,3,2,1,0:T(8,128)}) custom-call(s32[21]{0:T(128)} %stack.69.places._, f32[1024,8,128]{2,1,0:T(8,128)} %psf.1, bf16[4,128,128]{2,1,0:T(8,128)(2,1)} %constant.96.clone.pick), custom_call_target="tpu_custom_call" | custom-call | flops 536870912 | bytes 8388608 | tf_op jit(solution)/shard_map/psf_forward/pallas_call | solution.py:108
  26.6 52.3 %all-to-all-done = f32[128,32,256]{2,1,0:T(8,128)} async-done(((f32[128,32,256]{2,1,0:T(8,128)}), f32[128,32,256]{2,1,0:T(8,128)}, u32[]{:S(2)}, u32[]{:S(2)}) %all-to-all-start) | async-done | bytes 4194336 | tf_op jit(solution)/shard_map/all_to_all | solution.py:381
  78.9 6.1 %all-to-all-start.1 = ((f32[16,2,2,8,1024]{4,3,2,1,0:T(8,128)}), f32[16,2,2,8,1024]{4,3,2,1,0:T(8,128)S(1)}, u32[]{:S(2)}, u32[]{:S(2)}) async-start(f32[16,2,2,8,1024]{4,3,2,1,0:T(8,128)} %get-tuple-element.29), calls=%async_computation.1 | async-start | bytes 4194304 | tf_op jit(solution)/shard_map/all_to_all | solution.py:381
  85.0 11.7 %y_forward.1 = (f32[2,2,2,128,256]{4,3,2,1,0:T(8,128)}, f32[2,2,2,128,256]{4,3,2,1,0:T(8,128)}, f32[2,2,128,256]{3,2,1,0:T(8,128)}, f32[2,2,128,256]{3,2,1,0:T(8...) custom-call(s32[21]{0:T(128)} %stack.69.places._, f32[32,4,32,256]{3,2,1,0:T(8,128)} %bitcast.16.volume, ...), custom_call_target="tpu_custom_call" | custom-call | flops 6442450944 | bytes 12582912 | tf_op jit(solution)/shard_map/y_forward/pallas_call | solution.py:179
  96.7 1.0 collective-permute-start.1
  97.7 2.2 collective-permute-start.3
  99.9 10.1 %collective-permute-done.1.refs_0_ = f32[2,2,128,256]{3,2,1,0:T(8,128)S(1)} collective-permute-done((f32[2,2,128,256]{3,2,1,0:T(8,128)}, f32[2,2,128,256]{3,2,1,0:T(8,128)S(1)}, u32[]{:S(2)}, u32[]{:S(2)}) %collective-permute-start.1) | collective-permute-done | bytes 524320 | tf_op jit(solution)/shard_map/ppermute | solution.py:378
  110.1 0.8 copy-done.9
  110.9 2.5 all-to-all-done.1
  113.3 4.7 %all-to-all-start.2 = ((f32[16,2,2,8,1024]{4,3,2,1,0:T(8,128)}), f32[16,2,2,8,1024]{4,3,2,1,0:T(8,128)}, u32[]{:S(2)}, u32[]{:S(2)}) async-start(f32[16,2,2,8,1024]{4,3,2,1,0:T(8,128)} %get-tuple-element.30), calls=%async_computation.2 | async-start | bytes 4194304 | tf_op jit(solution)/shard_map/all_to_all | solution.py:381
  118.1 1.0 collective-permute-start.2
  119.2 2.6 collective-permute-start.4
  121.9 1.8 collective-permute-start.5
  124.0 10.2 %collective-permute-done.2.refs_1_ = f32[2,2,128,256]{3,2,1,0:T(8,128)S(1)} collective-permute-done((f32[2,2,128,256]{3,2,1,0:T(8,128)}, f32[2,2,128,256]{3,2,1,0:T(8,128)S(1)}, u32[]{:S(2)}, u32[]{:S(2)}) %collective-permute-start.2) | collective-permute-done | bytes 524320 | tf_op jit(solution)/shard_map/ppermute | solution.py:378
  134.3 0.9 copy-done.11
  135.2 1.0 copy-done.8
  136.3 11.6 %x_forward.1.spectrum = f32[2,2,2,128,1024]{4,3,2,1,0:T(8,128)} custom-call(s32[21]{0:T(128)} %stack.69.places._, f32[2,2,2,128,256]{4,3,2,1,0:T(8,128)} %get-tuple-element.21.own, f32[2,2,2,128,256]{4,3,2,1,0:T(8,128)} %copy-done.8, f32[2,2,128,256]{3,2,1,0:T(8,128)} %copy-done.9, f32[2,2,128,256]{3,2,1,0:T(8,128)} %copy-done.10, ...), custom_call_target="tpu_custom_call" | custom-call | flops 6442450944 | bytes 12582912 | tf_op jit(solution)/shard_map/x_forward/pallas_call | solution.py:210
  147.9 8.5 %collective-permute-done.5.above = f32[16,2,8,1024]{3,2,1,0:T(8,128)S(1)} collective-permute-done((f32[16,2,8,1024]{3,2,1,0:T(8,128)S(1)}, f32[16,2,8,1024]{3,2,1,0:T(8,128)S(1)}, u32[]{:S(2)}, u32[]{:S(2)}) %collective-permute-start.5) | collective-permute-done | bytes 1048608 | tf_op jit(solution)/shard_map/ppermute | solution.py:378
  156.4 1.0 copy-done.7
  157.4 13.7 %x_inverse.1 = (f32[2,2,2,128,256]{4,3,2,1,0:T(8,128)S(1)}, f32[2,2,2,128,256]{4,3,2,1,0:T(8,128)}, f32[2,2,128,256]{3,2,1,0:T(8,128)S(1)}, f32[2,2,128,256]{3,2...) custom-call(s32[21]{0:T(128)S(1)} %copy-done.3, ...), custom_call_target="tpu_custom_call" | custom-call | flops 6442450944 | bytes 16777216 | tf_op jit(solution)/shard_map/x_inverse/pallas_call | solution.py:264
  171.1 3.5 %collective-permute-start.10 = (f32[2,2,128,256]{3,2,1,0:T(8,128)S(1)}, f32[2,2,128,256]{3,2,1,0:T(8,128)S(1)}, u32[]{:S(2)}, u32[]{:S(2)}) collective-permute-start(f32[2,2,128,256]{3,2,1,0:T(8,128)S(1)} %get-tuple-element.35), channel_id=1, source_target_pairs={{0,18},{1,19},{2,0},{3,1},{16,2},{17,3},{18,16},{19,17},{4,22},{5,... | collective-permute-start | bytes 1572872 | tf_op jit(solution)/shard_map/ppermute | solution.py:378
  174.6 0.6 collective-permute-start.11
  175.3 1.2 collective-permute-start.8
  176.5 10.4 %collective-permute-done.10.refs_2_ = f32[2,2,128,256]{3,2,1,0:T(8,128)S(1)} collective-permute-done((f32[2,2,128,256]{3,2,1,0:T(8,128)S(1)}, f32[2,2,128,256]{3,2,1,0:T(8,128)S(1)}, u32[]{:S(2)}, u32[]{:S(2)}) %collective-permute-start.10) | collective-permute-done | bytes 524320 | tf_op jit(solution)/shard_map/ppermute | solution.py:378
  186.9 10.9 %collective-permute-done.11.refs_3_ = f32[2,2,128,256]{3,2,1,0:T(8,128)S(1)} collective-permute-done((f32[2,2,128,256]{3,2,1,0:T(8,128)S(1)}, f32[2,2,128,256]{3,2,1,0:T(8,128)S(1)}, u32[]{:S(2)}, u32[]{:S(2)}) %collective-permute-start.11) | collective-permute-done | bytes 524320 | tf_op jit(solution)/shard_map/ppermute | solution.py:378
  197.7 3.4 %collective-permute-done.9.refs_1_ = f32[2,2,128,256]{3,2,1,0:T(8,128)S(1)} collective-permute-done((f32[2,2,128,256]{3,2,1,0:T(8,128)S(1)}, f32[2,2,128,256]{3,2,1,0:T(8,128)S(1)}, u32[]{:S(2)}, u32[]{:S(2)}) %collective-permute-start.9) | collective-permute-done | bytes 524320 | tf_op jit(solution)/shard_map/ppermute | solution.py:378
  201.2 8.4 %y_inverse.1 = f32[32,4,32,256]{3,2,1,0:T(8,128)S(1)} custom-call(s32[21]{0:T(128)S(1)} %copy-done.3, f32[2,2,2,128,256]{4,3,2,1,0:T(8,128)S(1)} %get-tuple-element.31.own, f32[2,2,2,128,256]{4,3,2,1,0:T(8,128)S(1)} %collective-permute-done.7.across, f32[2,2,128,256]{3,2,1,0:T(8,128)S(1)} %collective-permute-done.8.refs_0_, ...), custom_call_target="tpu_custom_call" | custom-call | flops 6442450944 | bytes 12582912 | tf_op jit(solution)/shard_map/y_inverse/pallas_call | solution.py:304
  209.6 59.4 %all_to_all.20.volume = f32[128,32,256]{2,1,0:T(8,128)S(1)} all-to-all(f32[128,32,256]{2,1,0:T(8,128)S(1)} %bitcast.26), channel_id=1, replica_groups=mesh['x'=4,'zh'=2,'y'=4,'zl'=2,'core'=2] {'x','zh','y'}, dimensions={0} | all-to-all | bytes 8388608 | tf_op jit(solution)/shard_map/all_to_all | solution.py:381
  269.0 9.0 %z_inverse.1 = f32[256,32,128]{2,1,0:T(8,128)} custom-call(s32[1]{0:T(128)} %bitcast._, f32[128,32,256]{2,1,0:T(8,128)S(1)} %all_to_all.20.volume, f32[256,32,128]{2,1,0:T(8,128)S(1)} %copy-done, bf16[2,128,128]{2,1,0:T(8,128)(2,1)S(1)} %copy-done.1, bf16[2,128,128]{2,1,0:T(8,128)(2,1)S(1)} %copy-done.2), custom_call_target="tpu_custom_call" | custom-call | flops 805306368 | bytes 12582912 | tf_op jit(solution)/shard_map/z_inverse/pallas_call | solution.py:138
  (32 shorter events, 0.8 us)
Async XLA Ops:
  7.3 71.6 %all-to-all-start = ((f32[128,32,256]{2,1,0:T(8,128)}), f32[128,32,256]{2,1,0:T(8,128)}, u32[]{:S(2)}, u32[]{:S(2)}) async-start(f32[128,32,256]{2,1,0:T(8,128)} %z_forward.1), calls=%async_computation | async-start | bytes 8388608 | tf_op jit(solution)/shard_map/all_to_all | solution.py:381
  78.9 34.5 %all-to-all-start.1 = ((f32[16,2,2,8,1024]{4,3,2,1,0:T(8,128)}), f32[16,2,2,8,1024]{4,3,2,1,0:T(8,128)S(1)}, u32[]{:S(2)}, u32[]{:S(2)}) async-start(f32[16,2,2,8,1024]{4,3,2,1,0:T(8,128)} %get-tuple-element.29), calls=%async_computation.1 | async-start | bytes 4194304 | tf_op jit(solution)/shard_map/all_to_all | solution.py:381
  96.7 13.4 %collective-permute-start.1 = (f32[2,2,128,256]{3,2,1,0:T(8,128)}, f32[2,2,128,256]{3,2,1,0:T(8,128)S(1)}, u32[]{:S(2)}, u32[]{:S(2)}) collective-permute-start(f32[2,2,128,256]{3,2,1,0:T(8,128)} %get-tuple-element.23), channel_id=1, source_target_pairs={{0,2},{1,3},{2,16},{3,17},{16,18},{17,19},{18,0},{19,1},{4,6},{5,7... | collective-permute-start | bytes 1572872 | tf_op jit(solution)/shard_map/ppermute | solution.py:378
  97.7 13.2 %collective-permute-start.3 = (f32[2,2,128,256]{3,2,1,0:T(8,128)}, f32[2,2,128,256]{3,2,1,0:T(8,128)}, u32[]{:S(2)}, u32[]{:S(2)}) collective-permute-start(f32[2,2,128,256]{3,2,1,0:T(8,128)} %get-tuple-element.25), channel_id=1, source_target_pairs={{0,18},{1,19},{2,0},{3,1},{16,2},{17,3},{18,16},{19,17},{4,22},{5,... | collective-permute-start | bytes 1572872 | tf_op jit(solution)/shard_map/ppermute | solution.py:378
  110.1 0.8 copy-start.9
  113.3 4.7 %copy-start.6 = (f32[2,2,2,128,256]{4,3,2,1,0:T(8,128)S(1)}, f32[2,2,2,128,256]{4,3,2,1,0:T(8,128)}, u32[]{:S(2)}) copy-start(f32[2,2,2,128,256]{4,3,2,1,0:T(8,128)} %get-tuple-element.22) | copy-start | bytes 3145732
  113.3 44.1 %all-to-all-start.2 = ((f32[16,2,2,8,1024]{4,3,2,1,0:T(8,128)}), f32[16,2,2,8,1024]{4,3,2,1,0:T(8,128)}, u32[]{:S(2)}, u32[]{:S(2)}) async-start(f32[16,2,2,8,1024]{4,3,2,1,0:T(8,128)} %get-tuple-element.30), calls=%async_computation.2 | async-start | bytes 4194304 | tf_op jit(solution)/shard_map/all_to_all | solution.py:381
  118.0 16.3 %collective-permute-start = (f32[2,2,2,128,256]{4,3,2,1,0:T(8,128)S(1)}, f32[2,2,2,128,256]{4,3,2,1,0:T(8,128)S(1)}, u32[]{:S(2)}, u32[]{:S(2)}) collective-permute-start(f32[2,2,2,128,256]{4,3,2,1,0:T(8,128)S(1)} %copy-done.6), channel_id=1, source_target_pairs={{0,1},{1,0},{2,3},{3,2},{16,17},{17,16},{18,19},{19,18},{4,5},{5,4... | collective-permute-start | bytes 3145736 | tf_op jit(solution)/shard_map/ppermute | solution.py:378
  118.1 16.1 %collective-permute-start.2 = (f32[2,2,128,256]{3,2,1,0:T(8,128)}, f32[2,2,128,256]{3,2,1,0:T(8,128)S(1)}, u32[]{:S(2)}, u32[]{:S(2)}) collective-permute-start(f32[2,2,128,256]{3,2,1,0:T(8,128)} %get-tuple-element.24), channel_id=1, source_target_pairs={{0,3},{1,2},{2,17},{3,16},{16,19},{17,18},{18,1},{19,0},{4,7},{5,6... | collective-permute-start | bytes 1572872 | tf_op jit(solution)/shard_map/ppermute | solution.py:378
  119.2 15.2 %collective-permute-start.4 = (f32[2,2,128,256]{3,2,1,0:T(8,128)}, f32[2,2,128,256]{3,2,1,0:T(8,128)S(1)}, u32[]{:S(2)}, u32[]{:S(2)}) collective-permute-start(f32[2,2,128,256]{3,2,1,0:T(8,128)} %get-tuple-element.26), channel_id=1, source_target_pairs={{0,19},{1,18},{2,1},{3,0},{16,3},{17,2},{18,17},{19,16},{4,23},{5,... | collective-permute-start | bytes 1572872 | tf_op jit(solution)/shard_map/ppermute | solution.py:378
  121.9 34.5 %collective-permute-start.5 = (f32[16,2,8,1024]{3,2,1,0:T(8,128)S(1)}, f32[16,2,8,1024]{3,2,1,0:T(8,128)S(1)}, u32[]{:S(2)}, u32[]{:S(2)}) collective-permute-start(f32[16,2,8,1024]{3,2,1,0:T(8,128)S(1)} %get-tuple-element.38), channel_id=1, source_target_pairs={{0,18},{1,19},{2,0},{3,1},{16,2},{17,3},{18,16},{19,17},{4,22},{5,... | collective-permute-start | bytes 3145736 | tf_op jit(solution)/shard_map/ppermute | solution.py:378
  123.7 33.7 %collective-permute-start.6 = (f32[16,2,8,1024]{3,2,1,0:T(8,128)S(1)}, f32[16,2,8,1024]{3,2,1,0:T(8,128)}, u32[]{:S(2)}, u32[]{:S(2)}) collective-permute-start(f32[16,2,8,1024]{3,2,1,0:T(8,128)S(1)} %get-tuple-element.37), channel_id=1, source_target_pairs={{0,2},{1,3},{2,16},{3,17},{16,18},{17,19},{18,0},{19,1},{4,6},{5,7... | collective-permute-start | bytes 3145736 | tf_op jit(solution)/shard_map/ppermute | solution.py:378
  134.2 2.1 copy-start.10
  134.3 0.9 copy-start.11
  135.2 1.1 copy-start.8
  136.3 21.1 %copy-start.3 = (s32[21]{0:T(128)S(1)}, s32[21]{0:T(128)}, u32[]{:S(2)}) copy-start(s32[21]{0:T(128)} %stack.69.places._) | copy-start | bytes 256
  147.9 53.3 %copy-start.4 = (bf16[1024,1024]{1,0:T(8,128)(2,1)S(1)}, bf16[1024,1024]{1,0:T(8,128)(2,1)}, u32[]{:S(2)}) copy-start(bf16[1024,1024]{1,0:T(8,128)(2,1)} %constant.100.clone.refs_5_) | copy-start | bytes 6291460
  156.4 1.0 copy-start.7
  157.4 43.8 %copy-start.5 = (bf16[1024,1024]{1,0:T(8,128)(2,1)S(1)}, bf16[1024,1024]{1,0:T(8,128)(2,1)}, u32[]{:S(2)}) copy-start(bf16[1024,1024]{1,0:T(8,128)(2,1)} %constant.99.clone.refs_4_) | copy-start | bytes 6291460
  171.1 30.0 %collective-permute-start.7 = (f32[2,2,2,128,256]{4,3,2,1,0:T(8,128)}, f32[2,2,2,128,256]{4,3,2,1,0:T(8,128)S(1)}, u32[]{:S(2)}, u32[]{:S(2)}) collective-permute-start(f32[2,2,2,128,256]{4,3,2,1,0:T(8,128)} %get-tuple-element.32), channel_id=1, source_target_pairs={{0,1},{1,0},{2,3},{3,2},{16,17},{17,16},{18,19},{19,18},{4,5},{5,4... | collective-permute-start | bytes 3145736 | tf_op jit(solution)/shard_map/ppermute | solution.py:378
  171.1 15.8 %collective-permute-start.10 = (f32[2,2,128,256]{3,2,1,0:T(8,128)S(1)}, f32[2,2,128,256]{3,2,1,0:T(8,128)S(1)}, u32[]{:S(2)}, u32[]{:S(2)}) collective-permute-start(f32[2,2,128,256]{3,2,1,0:T(8,128)S(1)} %get-tuple-element.35), channel_id=1, source_target_pairs={{0,18},{1,19},{2,0},{3,1},{16,2},{17,3},{18,16},{19,17},{4,22},{5,... | collective-permute-start | bytes 1572872 | tf_op jit(solution)/shard_map/ppermute | solution.py:378
  174.6 23.1 %collective-permute-start.11 = (f32[2,2,128,256]{3,2,1,0:T(8,128)S(1)}, f32[2,2,128,256]{3,2,1,0:T(8,128)S(1)}, u32[]{:S(2)}, u32[]{:S(2)}) collective-permute-start(f32[2,2,128,256]{3,2,1,0:T(8,128)S(1)} %get-tuple-element.36), channel_id=1, source_target_pairs={{0,19},{1,18},{2,1},{3,0},{16,3},{17,2},{18,17},{19,16},{4,23},{5,... | collective-permute-start | bytes 1572872 | tf_op jit(solution)/shard_map/ppermute | solution.py:378
  175.3 22.5 %collective-permute-start.8 = (f32[2,2,128,256]{3,2,1,0:T(8,128)S(1)}, f32[2,2,128,256]{3,2,1,0:T(8,128)S(1)}, u32[]{:S(2)}, u32[]{:S(2)}) collective-permute-start(f32[2,2,128,256]{3,2,1,0:T(8,128)S(1)} %get-tuple-element.33), channel_id=1, source_target_pairs={{0,2},{1,3},{2,16},{3,17},{16,18},{17,19},{18,0},{19,1},{4,6},{5,7... | collective-permute-start | bytes 1572872 | tf_op jit(solution)/shard_map/ppermute | solution.py:378
  176.5 24.7 %collective-permute-start.9 = (f32[2,2,128,256]{3,2,1,0:T(8,128)S(1)}, f32[2,2,128,256]{3,2,1,0:T(8,128)S(1)}, u32[]{:S(2)}, u32[]{:S(2)}) collective-permute-start(f32[2,2,128,256]{3,2,1,0:T(8,128)S(1)} %get-tuple-element.34), channel_id=1, source_target_pairs={{0,3},{1,2},{2,17},{3,16},{16,19},{17,18},{18,1},{19,0},{4,7},{5,6... | collective-permute-start | bytes 1572872 | tf_op jit(solution)/shard_map/ppermute | solution.py:378
  209.6 59.5 %copy-start = (f32[256,32,128]{2,1,0:T(8,128)S(1)}, f32[256,32,128]{2,1,0:T(8,128)}, u32[]{:S(2)}) copy-start(f32[256,32,128]{2,1,0:T(8,128)} %estimate.1) | copy-start | bytes 12582916
  209.6 59.5 %copy-start.1 = (bf16[2,128,128]{2,1,0:T(8,128)(2,1)S(1)}, bf16[2,128,128]{2,1,0:T(8,128)(2,1)}, u32[]{:S(2)}) copy-start(bf16[2,128,128]{2,1,0:T(8,128)(2,1)} %constant.94.clone.high) | copy-start | bytes 196612
  209.6 59.4 %copy-start.2 = (bf16[2,128,128]{2,1,0:T(8,128)(2,1)S(1)}, bf16[2,128,128]{2,1,0:T(8,128)(2,1)}, u32[]{:S(2)}) copy-start(bf16[2,128,128]{2,1,0:T(8,128)(2,1)} %constant.95.clone.low) | copy-start | bytes 196612

commit v4 on v3

--- a/solution.py
+++ b/solution.py
@@ -398,7 +398,7 @@
         return own, send(across, 0, 1), from_below + from_above
 
     parts = exchange(*y_forward(places, volume, *y_rows))
-    near = first_all_to_all(after(near, (far, parts[2][0], parts[2][2])), ("x", "y"))
+    near = first_all_to_all(after(near, (far, parts[1], parts[2][0], parts[2][2])), ("x", "y"))
     above, below = send(far[:, 0], -1, 0), send(far[:, 1], 1, 0)
     spectrum = x_forward(places, *parts, *x_rows)
     parts = exchange(*x_inverse(places, spectrum, near, above, below, *x_columns))

time: 280 us -> 281 us (level)
  no operation moved by 1% of the time
where the time goes in v4:
time: 281 us
  waiting for transfers between devices  108 us (38%)
  Pallas kernels  69.3 us (25%)
  blocking collectives  60.1 us (21%)
  starting transfers between devices  37.9 us (13%)
  local copies, waits for them, and re-layouts  4.85 us (2%)
    all_to_all x1, blocking collectives, first_all_to_all(): return lax.all_to_all(value, axes, split_axis=0, concat_axis=0, tiled=True)  60.1 us
    ppermute x12, waiting for transfers between devices, send(): return lax.ppermute(value, ALL, moves(step, flip))  55.9 us
    all_to_all x3, waiting for transfers between devices, first_all_to_all(): return lax.all_to_all(value, axes, split_axis=0, concat_axis=0, tiled=True)  52.4 us
    all_to_all x3, starting transfers between devices, first_all_to_all(): return lax.all_to_all(value, axes, split_axis=0, concat_axis=0, tiled=True)  24.2 us
    pallas_call x1, Pallas kernels, x_inverse(): pl.pallas_call(x_inverse_kernel, grid_spec=pltpu.PrefetchScalarGridSpec(n...  13.7 us
    ppermute x12, starting transfers between devices, send(): return lax.ppermute(value, ALL, moves(step, flip))  13.7 us
    pallas_call x1, Pallas kernels, y_forward(): pl.pallas_call(y_forward_kernel, grid=(4,), in_specs=[SMEM, pl.BlockSpec(...  11.7 us
    pallas_call x1, Pallas kernels, x_forward(): pl.pallas_call(x_forward_kernel, grid=(4,), in_specs=[SMEM] + [pl.BlockSp...  11.6 us
  transfers between devices with their start and end apart: 15, of which 9 were waited for; matrix products, arithmetic and copies ran while one was open for 0% of the time, Pallas kernels for 11%

profile of v4, /device:TPU:0, one launch (start us, length us, event | category | flops | bytes accessed | tf_op | source)
XLA Modules:
  0.0 280.6 jit_solution(18257393466879587700)
XLA Ops:
  0.0 7.3 %z_forward.1 = f32[128,32,256]{2,1,0:T(8,128)} custom-call(s32[1]{0:T(128)} %bitcast._, f32[256,32,128]{2,1,0:T(8,128)} %volume.1, bf16[2,128,128]{2,1,0:T(8,128)(2,1)} %constant.94.clone.high, bf16[2,128,128]{2,1,0:T(8,128)(2,1)} %constant.95.clone.low), custom_call_target="tpu_custom_call" | custom-call | flops 805306368 | bytes 8388608 | tf_op jit(solution)/shard_map/z_forward/pallas_call | solution.py:80
  7.3 10.8 %all-to-all-start = ((f32[128,32,256]{2,1,0:T(8,128)}), f32[128,32,256]{2,1,0:T(8,128)}, u32[]{:S(2)}, u32[]{:S(2)}) async-start(f32[128,32,256]{2,1,0:T(8,128)} %z_forward.1), calls=%async_computation | async-start | bytes 8388608 | tf_op jit(solution)/shard_map/all_to_all | solution.py:381
  18.2 0.7 stack.69.places._
  18.8 7.7 %psf_forward.1 = (f32[16,2,2,8,1024]{4,3,2,1,0:T(8,128)}, f32[16,2,2,8,1024]{4,3,2,1,0:T(8,128)}) custom-call(s32[21]{0:T(128)} %stack.69.places._, f32[1024,8,128]{2,1,0:T(8,128)} %psf.1, bf16[4,128,128]{2,1,0:T(8,128)(2,1)} %constant.96.clone.pick), custom_call_target="tpu_custom_call" | custom-call | flops 536870912 | bytes 8388608 | tf_op jit(solution)/shard_map/psf_forward/pallas_call | solution.py:108
  26.5 52.4 %all-to-all-done = f32[128,32,256]{2,1,0:T(8,128)} async-done(((f32[128,32,256]{2,1,0:T(8,128)}), f32[128,32,256]{2,1,0:T(8,128)}, u32[]{:S(2)}, u32[]{:S(2)}) %all-to-all-start) | async-done | bytes 4194336 | tf_op jit(solution)/shard_map/all_to_all | solution.py:381
  78.9 6.1 %all-to-all-start.1 = ((f32[16,2,2,8,1024]{4,3,2,1,0:T(8,128)}), f32[16,2,2,8,1024]{4,3,2,1,0:T(8,128)S(1)}, u32[]{:S(2)}, u32[]{:S(2)}) async-start(f32[16,2,2,8,1024]{4,3,2,1,0:T(8,128)} %get-tuple-element.29), calls=%async_computation.1 | async-start | bytes 4194304 | tf_op jit(solution)/shard_map/all_to_all | solution.py:381
  85.0 11.7 %y_forward.1 = (f32[2,2,2,128,256]{4,3,2,1,0:T(8,128)}, f32[2,2,2,128,256]{4,3,2,1,0:T(8,128)}, f32[2,2,128,256]{3,2,1,0:T(8,128)}, f32[2,2,128,256]{3,2,1,0:T(8...) custom-call(s32[21]{0:T(128)} %stack.69.places._, f32[32,4,32,256]{3,2,1,0:T(8,128)} %bitcast.16.volume, ...), custom_call_target="tpu_custom_call" | custom-call | flops 6442450944 | bytes 12582912 | tf_op jit(solution)/shard_map/y_forward/pallas_call | solution.py:179
  96.7 1.1 collective-permute-start.1
  97.8 2.2 collective-permute-start.3
  100.0 12.5 %collective-permute-done.1.refs_0_ = f32[2,2,128,256]{3,2,1,0:T(8,128)S(1)} collective-permute-done((f32[2,2,128,256]{3,2,1,0:T(8,128)}, f32[2,2,128,256]{3,2,1,0:T(8,128)S(1)}, u32[]{:S(2)}, u32[]{:S(2)}) %collective-permute-start.1) | collective-permute-done | bytes 524320 | tf_op jit(solution)/shard_map/ppermute | solution.py:378
  112.5 0.8 copy-done.8
  113.3 0.8 copy-done.9
  114.1 1.0 copy-done.6
  115.0 7.3 %all-to-all-start.2 = ((f32[16,2,2,8,1024]{4,3,2,1,0:T(8,128)}), f32[16,2,2,8,1024]{4,3,2,1,0:T(8,128)}, u32[]{:S(2)}, u32[]{:S(2)}) async-start(f32[16,2,2,8,1024]{4,3,2,1,0:T(8,128)} %get-tuple-element.30), calls=%async_computation.2 | async-start | bytes 4194304 | tf_op jit(solution)/shard_map/all_to_all | solution.py:381
  122.4 2.9 %collective-permute-start.4 = (f32[2,2,128,256]{3,2,1,0:T(8,128)}, f32[2,2,128,256]{3,2,1,0:T(8,128)S(1)}, u32[]{:S(2)}, u32[]{:S(2)}) collective-permute-start(f32[2,2,128,256]{3,2,1,0:T(8,128)} %get-tuple-element.26), channel_id=1, source_target_pairs={{0,19},{1,18},{2,1},{3,0},{16,3},{17,2},{18,17},{19,16},{4,23},{5,... | collective-permute-start | bytes 1572872 | tf_op jit(solution)/shard_map/ppermute | solution.py:378
  125.5 1.0 collective-permute-start.5
  126.5 1.1 collective-permute-start.6
  127.6 10.4 %collective-permute-done.2.refs_1_ = f32[2,2,128,256]{3,2,1,0:T(8,128)S(1)} collective-permute-done((f32[2,2,128,256]{3,2,1,0:T(8,128)}, f32[2,2,128,256]{3,2,1,0:T(8,128)S(1)}, u32[]{:S(2)}, u32[]{:S(2)}) %collective-permute-start.2) | collective-permute-done | bytes 524320 | tf_op jit(solution)/shard_map/ppermute | solution.py:378
  138.0 0.8 copy-done.10
  139.0 11.6 %x_forward.1.spectrum = f32[2,2,2,128,1024]{4,3,2,1,0:T(8,128)} custom-call(s32[21]{0:T(128)} %stack.69.places._, f32[2,2,2,128,256]{4,3,2,1,0:T(8,128)} %get-tuple-element.21.own, f32[2,2,2,128,256]{4,3,2,1,0:T(8,128)} %copy-done.6, f32[2,2,128,256]{3,2,1,0:T(8,128)} %copy-done.8, f32[2,2,128,256]{3,2,1,0:T(8,128)} %copy-done.10, ...), custom_call_target="tpu_custom_call" | custom-call | flops 6442450944 | bytes 12582912 | tf_op jit(solution)/shard_map/x_forward/pallas_call | solution.py:210
  150.6 8.8 %collective-permute-done.5.above = f32[16,2,8,1024]{3,2,1,0:T(8,128)S(1)} collective-permute-done((f32[16,2,8,1024]{3,2,1,0:T(8,128)S(1)}, f32[16,2,8,1024]{3,2,1,0:T(8,128)S(1)}, u32[]{:S(2)}, u32[]{:S(2)}) %collective-permute-start.5) | collective-permute-done | bytes 1048608 | tf_op jit(solution)/shard_map/ppermute | solution.py:378
  159.4 0.4 collective-permute-done.6.below
  159.8 0.5 copy-done.7
  160.3 13.7 %x_inverse.1 = (f32[2,2,2,128,256]{4,3,2,1,0:T(8,128)S(1)}, f32[2,2,2,128,256]{4,3,2,1,0:T(8,128)}, f32[2,2,128,256]{3,2,1,0:T(8,128)S(1)}, f32[2,2,128,256]{3,2...) custom-call(s32[21]{0:T(128)S(1)} %copy-done.3, ...), custom_call_target="tpu_custom_call" | custom-call | flops 6442450944 | bytes 16777216 | tf_op jit(solution)/shard_map/x_inverse/pallas_call | solution.py:264
  174.2 3.2 %collective-permute-start.10 = (f32[2,2,128,256]{3,2,1,0:T(8,128)S(1)}, f32[2,2,128,256]{3,2,1,0:T(8,128)S(1)}, u32[]{:S(2)}, u32[]{:S(2)}) collective-permute-start(f32[2,2,128,256]{3,2,1,0:T(8,128)S(1)} %get-tuple-element.35), channel_id=1, source_target_pairs={{0,18},{1,19},{2,0},{3,1},{16,2},{17,3},{18,16},{19,17},{4,22},{5,... | collective-permute-start | bytes 1572872 | tf_op jit(solution)/shard_map/ppermute | solution.py:378
  177.6 1.7 collective-permute-start.8
  179.3 10.4 %collective-permute-done.10.refs_2_ = f32[2,2,128,256]{3,2,1,0:T(8,128)S(1)} collective-permute-done((f32[2,2,128,256]{3,2,1,0:T(8,128)S(1)}, f32[2,2,128,256]{3,2,1,0:T(8,128)S(1)}, u32[]{:S(2)}, u32[]{:S(2)}) %collective-permute-start.10) | collective-permute-done | bytes 524320 | tf_op jit(solution)/shard_map/ppermute | solution.py:378
  189.6 10.9 %collective-permute-done.11.refs_3_ = f32[2,2,128,256]{3,2,1,0:T(8,128)S(1)} collective-permute-done((f32[2,2,128,256]{3,2,1,0:T(8,128)S(1)}, f32[2,2,128,256]{3,2,1,0:T(8,128)S(1)}, u32[]{:S(2)}, u32[]{:S(2)}) %collective-permute-start.11) | collective-permute-done | bytes 524320 | tf_op jit(solution)/shard_map/ppermute | solution.py:378
  200.5 2.6 collective-permute-done.9.refs_1_
  203.1 8.4 %y_inverse.1 = f32[32,4,32,256]{3,2,1,0:T(8,128)S(1)} custom-call(s32[21]{0:T(128)S(1)} %copy-done.3, f32[2,2,2,128,256]{4,3,2,1,0:T(8,128)S(1)} %get-tuple-element.31.own, f32[2,2,2,128,256]{4,3,2,1,0:T(8,128)S(1)} %collective-permute-done.7.across, f32[2,2,128,256]{3,2,1,0:T(8,128)S(1)} %collective-permute-done.8.refs_0_, ...), custom_call_target="tpu_custom_call" | custom-call | flops 6442450944 | bytes 12582912 | tf_op jit(solution)/shard_map/y_inverse/pallas_call | solution.py:304
  211.5 60.1 %all_to_all.20.volume = f32[128,32,256]{2,1,0:T(8,128)S(1)} all-to-all(f32[128,32,256]{2,1,0:T(8,128)S(1)} %bitcast.26), channel_id=1, replica_groups=mesh['x'=4,'zh'=2,'y'=4,'zl'=2,'core'=2] {'x','zh','y'}, dimensions={0} | all-to-all | bytes 8388608 | tf_op jit(solution)/shard_map/all_to_all | solution.py:381
  271.6 9.0 %z_inverse.1 = f32[256,32,128]{2,1,0:T(8,128)} custom-call(s32[1]{0:T(128)} %bitcast._, f32[128,32,256]{2,1,0:T(8,128)S(1)} %all_to_all.20.volume, f32[256,32,128]{2,1,0:T(8,128)S(1)} %copy-done, bf16[2,128,128]{2,1,0:T(8,128)(2,1)S(1)} %copy-done.1, bf16[2,128,128]{2,1,0:T(8,128)(2,1)S(1)} %copy-done.2), custom_call_target="tpu_custom_call" | custom-call | flops 805306368 | bytes 12582912 | tf_op jit(solution)/shard_map/z_inverse/pallas_call | solution.py:138
  (32 shorter events, 0.9 us)
Async XLA Ops:
  7.3 71.6 %all-to-all-start = ((f32[128,32,256]{2,1,0:T(8,128)}), f32[128,32,256]{2,1,0:T(8,128)}, u32[]{:S(2)}, u32[]{:S(2)}) async-start(f32[128,32,256]{2,1,0:T(8,128)} %z_forward.1), calls=%async_computation | async-start | bytes 8388608 | tf_op jit(solution)/shard_map/all_to_all | solution.py:381
  78.9 35.2 %all-to-all-start.1 = ((f32[16,2,2,8,1024]{4,3,2,1,0:T(8,128)}), f32[16,2,2,8,1024]{4,3,2,1,0:T(8,128)S(1)}, u32[]{:S(2)}, u32[]{:S(2)}) async-start(f32[16,2,2,8,1024]{4,3,2,1,0:T(8,128)} %get-tuple-element.29), calls=%async_computation.1 | async-start | bytes 4194304 | tf_op jit(solution)/shard_map/all_to_all | solution.py:381
  96.7 17.4 %collective-permute-start = (f32[2,2,2,128,256]{4,3,2,1,0:T(8,128)}, f32[2,2,2,128,256]{4,3,2,1,0:T(8,128)S(1)}, u32[]{:S(2)}, u32[]{:S(2)}) collective-permute-start(f32[2,2,2,128,256]{4,3,2,1,0:T(8,128)} %get-tuple-element.22), channel_id=1, source_target_pairs={{0,1},{1,0},{2,3},{3,2},{16,17},{17,16},{18,19},{19,18},{4,5},{5,4... | collective-permute-start | bytes 3145736 | tf_op jit(solution)/shard_map/ppermute | solution.py:378
  96.7 15.8 %collective-permute-start.1 = (f32[2,2,128,256]{3,2,1,0:T(8,128)}, f32[2,2,128,256]{3,2,1,0:T(8,128)S(1)}, u32[]{:S(2)}, u32[]{:S(2)}) collective-permute-start(f32[2,2,128,256]{3,2,1,0:T(8,128)} %get-tuple-element.23), channel_id=1, source_target_pairs={{0,2},{1,3},{2,16},{3,17},{16,18},{17,19},{18,0},{19,1},{4,6},{5,7... | collective-permute-start | bytes 1572872 | tf_op jit(solution)/shard_map/ppermute | solution.py:378
  97.8 14.7 %collective-permute-start.3 = (f32[2,2,128,256]{3,2,1,0:T(8,128)}, f32[2,2,128,256]{3,2,1,0:T(8,128)S(1)}, u32[]{:S(2)}, u32[]{:S(2)}) collective-permute-start(f32[2,2,128,256]{3,2,1,0:T(8,128)} %get-tuple-element.25), channel_id=1, source_target_pairs={{0,18},{1,19},{2,0},{3,1},{16,2},{17,3},{18,16},{19,17},{4,22},{5,... | collective-permute-start | bytes 1572872 | tf_op jit(solution)/shard_map/ppermute | solution.py:378
  112.5 0.8 copy-start.8
  113.3 0.8 copy-start.9
  114.1 1.0 copy-start.6
  115.0 44.8 %all-to-all-start.2 = ((f32[16,2,2,8,1024]{4,3,2,1,0:T(8,128)}), f32[16,2,2,8,1024]{4,3,2,1,0:T(8,128)}, u32[]{:S(2)}, u32[]{:S(2)}) async-start(f32[16,2,2,8,1024]{4,3,2,1,0:T(8,128)} %get-tuple-element.30), calls=%async_computation.2 | async-start | bytes 4194304 | tf_op jit(solution)/shard_map/all_to_all | solution.py:381
  122.3 15.6 %collective-permute-start.2 = (f32[2,2,128,256]{3,2,1,0:T(8,128)}, f32[2,2,128,256]{3,2,1,0:T(8,128)S(1)}, u32[]{:S(2)}, u32[]{:S(2)}) collective-permute-start(f32[2,2,128,256]{3,2,1,0:T(8,128)} %get-tuple-element.24), channel_id=1, source_target_pairs={{0,3},{1,2},{2,17},{3,16},{16,19},{17,18},{18,1},{19,0},{4,7},{5,6... | collective-permute-start | bytes 1572872 | tf_op jit(solution)/shard_map/ppermute | solution.py:378
  122.4 15.6 %collective-permute-start.4 = (f32[2,2,128,256]{3,2,1,0:T(8,128)}, f32[2,2,128,256]{3,2,1,0:T(8,128)S(1)}, u32[]{:S(2)}, u32[]{:S(2)}) collective-permute-start(f32[2,2,128,256]{3,2,1,0:T(8,128)} %get-tuple-element.26), channel_id=1, source_target_pairs={{0,19},{1,18},{2,1},{3,0},{16,3},{17,2},{18,17},{19,16},{4,23},{5,... | collective-permute-start | bytes 1572872 | tf_op jit(solution)/shard_map/ppermute | solution.py:378
  125.5 33.9 %collective-permute-start.5 = (f32[16,2,8,1024]{3,2,1,0:T(8,128)S(1)}, f32[16,2,8,1024]{3,2,1,0:T(8,128)S(1)}, u32[]{:S(2)}, u32[]{:S(2)}) collective-permute-start(f32[16,2,8,1024]{3,2,1,0:T(8,128)S(1)} %get-tuple-element.38), channel_id=1, source_target_pairs={{0,18},{1,19},{2,0},{3,1},{16,2},{17,3},{18,16},{19,17},{4,22},{5,... | collective-permute-start | bytes 3145736 | tf_op jit(solution)/shard_map/ppermute | solution.py:378
  126.5 33.3 %collective-permute-start.6 = (f32[16,2,8,1024]{3,2,1,0:T(8,128)S(1)}, f32[16,2,8,1024]{3,2,1,0:T(8,128)}, u32[]{:S(2)}, u32[]{:S(2)}) collective-permute-start(f32[16,2,8,1024]{3,2,1,0:T(8,128)S(1)} %get-tuple-element.37), channel_id=1, source_target_pairs={{0,2},{1,3},{2,16},{3,17},{16,18},{17,19},{18,0},{19,1},{4,6},{5,7... | collective-permute-start | bytes 3145736 | tf_op jit(solution)/shard_map/ppermute | solution.py:378
  137.9 0.8 copy-start.10
  138.0 1.0 copy-start.11
  139.0 21.4 %copy-start.3 = (s32[21]{0:T(128)S(1)}, s32[21]{0:T(128)}, u32[]{:S(2)}) copy-start(s32[21]{0:T(128)} %stack.69.places._) | copy-start | bytes 256
  150.6 52.5 %copy-start.4 = (bf16[1024,1024]{1,0:T(8,128)(2,1)S(1)}, bf16[1024,1024]{1,0:T(8,128)(2,1)}, u32[]{:S(2)}) copy-start(bf16[1024,1024]{1,0:T(8,128)(2,1)} %constant.100.clone.refs_5_) | copy-start | bytes 6291460
  159.4 1.0 copy-start.7
  160.3 42.8 %copy-start.5 = (bf16[1024,1024]{1,0:T(8,128)(2,1)S(1)}, bf16[1024,1024]{1,0:T(8,128)(2,1)}, u32[]{:S(2)}) copy-start(bf16[1024,1024]{1,0:T(8,128)(2,1)} %constant.99.clone.refs_4_) | copy-start | bytes 6291460
  174.0 29.0 %collective-permute-start.7 = (f32[2,2,2,128,256]{4,3,2,1,0:T(8,128)}, f32[2,2,2,128,256]{4,3,2,1,0:T(8,128)S(1)}, u32[]{:S(2)}, u32[]{:S(2)}) collective-permute-start(f32[2,2,2,128,256]{4,3,2,1,0:T(8,128)} %get-tuple-element.32), channel_id=1, source_target_pairs={{0,1},{1,0},{2,3},{3,2},{16,17},{17,16},{18,19},{19,18},{4,5},{5,4... | collective-permute-start | bytes 3145736 | tf_op jit(solution)/shard_map/ppermute | solution.py:378
  174.2 15.4 %collective-permute-start.10 = (f32[2,2,128,256]{3,2,1,0:T(8,128)S(1)}, f32[2,2,128,256]{3,2,1,0:T(8,128)S(1)}, u32[]{:S(2)}, u32[]{:S(2)}) collective-permute-start(f32[2,2,128,256]{3,2,1,0:T(8,128)S(1)} %get-tuple-element.35), channel_id=1, source_target_pairs={{0,18},{1,19},{2,0},{3,1},{16,2},{17,3},{18,16},{19,17},{4,22},{5,... | collective-permute-start | bytes 1572872 | tf_op jit(solution)/shard_map/ppermute | solution.py:378
  177.4 23.1 %collective-permute-start.11 = (f32[2,2,128,256]{3,2,1,0:T(8,128)S(1)}, f32[2,2,128,256]{3,2,1,0:T(8,128)S(1)}, u32[]{:S(2)}, u32[]{:S(2)}) collective-permute-start(f32[2,2,128,256]{3,2,1,0:T(8,128)S(1)} %get-tuple-element.36), channel_id=1, source_target_pairs={{0,19},{1,18},{2,1},{3,0},{16,3},{17,2},{18,17},{19,16},{4,23},{5,... | collective-permute-start | bytes 1572872 | tf_op jit(solution)/shard_map/ppermute | solution.py:378
  177.6 23.0 %collective-permute-start.8 = (f32[2,2,128,256]{3,2,1,0:T(8,128)S(1)}, f32[2,2,128,256]{3,2,1,0:T(8,128)S(1)}, u32[]{:S(2)}, u32[]{:S(2)}) collective-permute-start(f32[2,2,128,256]{3,2,1,0:T(8,128)S(1)} %get-tuple-element.33), channel_id=1, source_target_pairs={{0,2},{1,3},{2,16},{3,17},{16,18},{17,19},{18,0},{19,1},{4,6},{5,7... | collective-permute-start | bytes 1572872 | tf_op jit(solution)/shard_map/ppermute | solution.py:378
  179.3 23.8 %collective-permute-start.9 = (f32[2,2,128,256]{3,2,1,0:T(8,128)S(1)}, f32[2,2,128,256]{3,2,1,0:T(8,128)S(1)}, u32[]{:S(2)}, u32[]{:S(2)}) collective-permute-start(f32[2,2,128,256]{3,2,1,0:T(8,128)S(1)} %get-tuple-element.34), channel_id=1, source_target_pairs={{0,3},{1,2},{2,17},{3,16},{16,19},{17,18},{18,1},{19,0},{4,7},{5,6... | collective-permute-start | bytes 1572872 | tf_op jit(solution)/shard_map/ppermute | solution.py:378
  211.5 60.1 %copy-start = (f32[256,32,128]{2,1,0:T(8,128)S(1)}, f32[256,32,128]{2,1,0:T(8,128)}, u32[]{:S(2)}) copy-start(f32[256,32,128]{2,1,0:T(8,128)} %estimate.1) | copy-start | bytes 12582916
  211.5 60.1 %copy-start.1 = (bf16[2,128,128]{2,1,0:T(8,128)(2,1)S(1)}, bf16[2,128,128]{2,1,0:T(8,128)(2,1)}, u32[]{:S(2)}) copy-start(bf16[2,128,128]{2,1,0:T(8,128)(2,1)} %constant.94.clone.high) | copy-start | bytes 196612
  211.5 60.1 %copy-start.2 = (bf16[2,128,128]{2,1,0:T(8,128)(2,1)S(1)}, bf16[2,128,128]{2,1,0:T(8,128)(2,1)}, u32[]{:S(2)}) copy-start(bf16[2,128,128]{2,1,0:T(8,128)(2,1)} %constant.95.clone.low) | copy-start | bytes 196612
